TPU v7x, 128 devices: a whole 4x4x4 slice. The times are simulated.
128 devices in a mesh: ep: 32 (over y, z, core), tp: 4 (over x).
Axes of the slice: x: 4, y: 4, z: 4, core: 2. Of those that a mesh axis runs over, the one named last changes fastest.
Arguments:
- tokens: bfloat16 [4096, 4096], P('ep', 'tp'), may hold values from -6 to 6
- keep_mask: int32 [4096], P('ep'), may hold values 0 or 1
- expert_ids: int32 [4096, 8], P('ep'), may hold values from 0 to 63, all different within a row; in each aligned block of 128 rows (0 to 127, 128 to 255, ...) at most 32 rows name the same one
- route_weight: float32 [4096, 8], P('ep'), may hold values from 0.1 to 1
- w_gate: bfloat16 [64, 4096, 1536], P('ep', None, 'tp'), may hold values from -0.09375 to 0.09375
- w_up: bfloat16 [64, 4096, 1536], P('ep', None, 'tp'), may hold values from -0.09375 to 0.09375
- w_down: bfloat16 [64, 1536, 4096], P('ep', 'tp'), may hold values from -0.15625 to 0.15625
- norm_gain: float32 [4096], replicated, may hold values from 0.1 to 1.9
- kv_weight: bfloat16 [4096, 1024], P(None, 'tp'), may hold values from -0.09375 to 0.09375
Outputs:
- mixed_out: bfloat16 [4096, 4096], P('ep', 'tp')
- kv_rows: bfloat16 [4096, 1024], P('ep', 'tp')
Inputs may be any that keep to these rules, and one draw needn't show every extreme that they name: `expert_ids`: within the rows of one device (128 rows, aligned blocks) no expert is named by more than 32 rows, a bound that some block reaches; a row names 8 different experts.
All inputs are finite; a program needn't handle non-finite values. No bound on the sum of `keep_mask` on one device may be relied on, other than what follows from the above.
Results may differ from a plain program's by a relative error of at most 0.014.
Values may be sent and summed in bfloat16 or wider, within the bound.
No kernel may reach another device: no remote copies, remote signals or barrier semaphores. Data moves between devices by JAX's collectives and lax.ppermute only.
A program may use at most 128 MiB of HBM per device.

v0:
```python
import jax
import jax.numpy as jnp
from jax import lax
from jax.sharding import PartitionSpec as P


def on_device(
    tokens, keep_mask, expert_ids, route_weight, w_gate, w_up, w_down, norm_gain, kv_weight
):
    tok_rows, slice_width = tokens.shape
    top_k = expert_ids.shape[1]
    ep_count = lax.axis_size("ep")
    local_experts = w_gate.shape[0]
    all_experts = local_experts * ep_count
    capacity = 2 * tok_rows * top_k // all_experts
    flat_expert = expert_ids.reshape(-1)
    active = jnp.repeat(keep_mask, top_k) > 0
    onehot = (
        (flat_expert[:, None] == jnp.arange(all_experts, dtype=jnp.int32)[None, :])
        & active[:, None]
    ).astype(jnp.int32)
    before = jnp.cumsum(onehot, axis=0) - onehot
    slot_idx = jnp.sum(before * onehot, axis=1)
    target = jnp.where(active, flat_expert * capacity + slot_idx, all_experts * capacity)
    counts = jnp.sum(onehot, axis=0)
    count_sent = counts.reshape(ep_count, local_experts).astype(jnp.bfloat16)
    source_row = jnp.arange(tok_rows * top_k, dtype=jnp.int32) // top_k
    full_rows = lax.all_gather(tokens, "tp", axis=1, tiled=True)
    picked = full_rows[source_row]
    empty = jnp.zeros((all_experts * capacity, full_rows.shape[1]), full_rows.dtype)
    arrived = lax.all_to_all(
        empty.at[target].set(picked, mode="drop"), "ep", split_axis=0, concat_axis=0, tiled=True
    )
    got_sent = lax.all_to_all(count_sent, "ep", split_axis=0, concat_axis=0, tiled=True)
    got_counts = got_sent.astype(jnp.int32)
    feat_width = arrived.shape[1]
    slot_rows = arrived.reshape(ep_count, local_experts, capacity, feat_width)
    gate_val = jnp.einsum("secd,edf->secf", slot_rows, w_gate, preferred_element_type=jnp.float32)
    up_val = jnp.einsum("secd,edf->secf", slot_rows, w_up, preferred_element_type=jnp.float32)
    usable = jnp.arange(capacity, dtype=jnp.int32)[None, None, :] < got_counts[:, :, None]
    hidden = jnp.where(usable[..., None], jax.nn.silu(gate_val) * up_val, 0.0).astype(jnp.bfloat16)
    partial_value = jnp.einsum("secf,efd->secd", hidden, w_down, preferred_element_type=jnp.float32)
    reduced = lax.psum_scatter(
        partial_value.astype(jnp.bfloat16), "tp", scatter_dimension=3, tiled=True
    )
    returned = lax.all_to_all(
        reduced.reshape(all_experts * capacity, slice_width),
        "ep",
        split_axis=0,
        concat_axis=0,
        tiled=True,
    )
    picked = jnp.take(returned, jnp.minimum(target, all_experts * capacity - 1), axis=0).astype(
        jnp.float32
    )
    weights = jnp.where(active, route_weight.reshape(-1), 0.0)
    summed = jnp.sum((weights[:, None] * picked).reshape(tok_rows, top_k, slice_width), axis=1)
    mixed_out = (tokens.astype(jnp.float32) + summed).astype(jnp.bfloat16)
    gathered = lax.all_gather(mixed_out, "tp", axis=1, tiled=True).astype(jnp.float32)
    mean_square = jnp.mean(gathered * gathered, axis=-1, keepdims=True)
    normed = (gathered * lax.rsqrt(mean_square + 1e-06) * norm_gain).astype(jnp.bfloat16)
    kv_rows = jnp.dot(normed, kv_weight, preferred_element_type=jnp.float32).astype(jnp.bfloat16)
    return (mixed_out, kv_rows)


def solution(mesh):
    in_specs = (
        P("ep", "tp"),
        P("ep"),
        P("ep", None),
        P("ep", None),
        P("ep", None, "tp"),
        P("ep", None, "tp"),
        P("ep", "tp", None),
        P(),
        P(None, "tp"),
    )
    out_specs = (P("ep", "tp"), P("ep", "tp"))
    return jax.shard_map(
        on_device, mesh=mesh, in_specs=in_specs, out_specs=out_specs, check_vma=False
    )
```

profile of v0, /device:TPU:0, one launch (start us, length us, event | category | flops | bytes accessed | tf_op | source)
XLA Modules:
  0.0 655.7 jit_solution(2803440812167379393)
XLA Ops:
  7.2 0.0 all-gather.3.cloned.1.call-start
  7.2 0.7 all-gather.3.cloned.1.call-update
  7.9 0.8 copy.39
  8.7 0.1 eq.26
  8.8 0.1 reshape.223
  8.9 0.7 broadcast_compare_fusion
  9.5 0.1 gt.43
  9.6 0.1 broadcast_in_dim.52
  9.7 0.1 gt.44
  9.9 18.0 %reduce-window.6 = s32[64,8,128]{2,1,0:T(8,128)S(1)} reduce-window(s32[64,8,128]{2,1,0:T(8,128)S(1)} %fusion.35, s32[]{:T(128)} %constant.25.clone.1), window={size=1x1x128 pad=0_0x0_0x127_0}, to_apply=%region_0.0 | reduce-window | flops 8323072 | bytes 524292 | tf_op jit(solution)/shard_map/reduce-window
  27.9 0.1 slice.12
  28.0 0.1 copy.42
  28.2 0.1 copy.43
  28.3 0.1 broadcast_in_dim.50.clone
  28.4 0.1 gt.42
  28.5 0.1 broadcast_add_fusion
  28.6 0.2 convert_reduce_fusion
  28.8 0.7 convert_element_type.74
  29.6 8.4 %all-to-all-start = ((bf16[32,1,2]{2,1,0:T(2,128)(2,1)}), bf16[32,1,2]{2,1,0:T(2,128)(2,1)S(1)}, u32[]{:S(2)}, u32[]{:S(2)}) async-start(bf16[32,1,2]{2,1,0:T(2,128)(2,1)} %convert_element_type.74), calls=%async_computation | async-start | bytes 32768 | tf_op jit(solution)/shard_map/all_to_all | solution.py:34
  38.0 0.1 gt.45
  38.1 0.7 broadcast_multiply_fusion
  38.8 0.1 copy.49
  38.9 0.1 mul.65
  39.0 0.0 all-gather.3.cloned.1.call-done
  39.1 16.4 %gather_fusion = bf16[1024,4096]{1,0:T(8,128)(2,1)} fusion(bf16[128,4096]{1,0:T(8,128)(2,1)} %all-gather.3.cloned.1.call-done, s32[1024]{0:T(1024)S(1)} %broadcast_clamp_fusion.1), kind=kCustom, calls=%fused_computation | custom fusion | bytes 16781312 | tf_op jit(solution)/shard_map/gather | solution.py:29
  55.5 22.0 %scatter_custom_fusion = bf16[2048,4096]{1,0:T(8,128)(2,1)} fusion(s32[1024]{0:T(1024)S(1)} %bitcast.77, bf16[1024,4096]{1,0:T(8,128)(2,1)} %gather_fusion, bf16[]{:T(256)} %constant.48.clone.1), kind=kCustom, calls=%fused_computation.8 | custom fusion | bytes 16777728 | tf_op jit(solution)/shard_map/scatter | solution.py:32
  77.5 7.5 %all-to-all-start.1 = ((bf16[32,64,4096]{2,1,0:T(8,128)(2,1)}), bf16[32,64,4096]{2,1,0:T(8,128)(2,1)}, u32[]{:S(2)}, u32[]{:S(2)}) async-start(bf16[32,64,4096]{2,1,0:T(8,128)(2,1)} %bitcast.70), calls=%async_computation.1 | async-start | bytes 33554432 | tf_op jit(solution)/shard_map/all_to_all | solution.py:31
  85.0 0.0 reduce-scatter.2.cloned.1.call-start
  85.0 0.1 copy.47
  85.1 0.1 iota_compare_fusion.2
  85.2 240.7 %all-to-all-done.1 = bf16[32,64,4096]{2,1,0:T(8,128)(2,1)} async-done(((bf16[32,64,4096]{2,1,0:T(8,128)(2,1)}), bf16[32,64,4096]{2,1,0:T(8,128)(2,1)}, u32[]{:S(2)}, u32[]{:S(2)}) %all-to-all-start.1) | async-done | bytes 16777248 | tf_op jit(solution)/shard_map/all_to_all | solution.py:31
  325.9 15.4 %fusion.2 = f32[2,32,32,384]{3,2,1,0:T(8,128)} fusion(bf16[32,2,32,4096]{3,2,1,0:T(8,128)(2,1)} %bitcast.7, bf16[2,4096,384]{2,1,0:T(8,128)(2,1)} %param.13), kind=kOutput, calls=%fused_computation.6 | convolution fusion | flops 6442450944 | bytes 26214400 | tf_op jit(solution)/shard_map/secd,edf->secf/dot_general | solution.py:38
  341.2 26.2 %convert_bitcast_fusion = bf16[32,2,32,4096]{3,2,0,1:T(8,128)(2,1)} fusion(bf16[2,384,4096]{2,1,0:T(8,128)(2,1)} %param.15, f32[2,32,32,384]{3,2,1,0:T(8,128)} %fusion.2, bf16[2,4096,384]{2,1,0:T(8,128)(2,1)} %param.14, bf16[32,2,32,4096]{3,2,1,0:T(8,128)(2,1)} %bitcast.7, pred[32,2,32]{2,0,1:T(8,128)(4,1)S(1)} %iota_compare_fusion.2), kind=kOutput, calls=%fused_computation.3 | convolution fusion | flops 12898795520 | bytes 49285120 | tf_op jit(solution)/shard_map/secf,efd->secd/dot_general | solution.py:42
  367.5 0.0 reduce-scatter.2.cloned.1.call-update
  367.5 176.7 %reduce-scatter.2.cloned.1.call-done = bf16[32,2,32,1024]{3,2,0,1:T(8,128)(2,1)} async-done(((bf16[32,2,32,4096]{3,2,0,1:T(8,128)(2,1)}), bf16[32,2,32,1024]{3,2,0,1:T(8,128)(2,1)}) %reduce-scatter.2.cloned.1.call-update) | async-done | bytes 4194320 | tf_op jit(solution)/shard_map/reduce_scatter | solution.py:43
  544.2 5.0 copy.52
  549.2 7.5 %all-to-all-start.2 = ((bf16[32,64,1024]{2,1,0:T(8,128)(2,1)}), bf16[32,64,1024]{2,1,0:T(8,128)(2,1)}, u32[]{:S(2)}, u32[]{:S(2)}) async-start(bf16[32,64,1024]{2,1,0:T(8,128)(2,1)} %bitcast.71), calls=%async_computation.3 | async-start | bytes 8388608 | tf_op jit(solution)/shard_map/all_to_all | solution.py:46
  556.7 0.0 all-gather.5.cloned.1.call-start
  556.8 0.1 reduce_sum.41
  556.9 0.1 copy.45
  557.1 0.1 copy.38
  557.2 52.3 %all-to-all-done.2 = bf16[32,64,1024]{2,1,0:T(8,128)(2,1)} async-done(((bf16[32,64,1024]{2,1,0:T(8,128)(2,1)}), bf16[32,64,1024]{2,1,0:T(8,128)(2,1)}, u32[]{:S(2)}, u32[]{:S(2)}) %all-to-all-start.2) | async-done | bytes 4194336 | tf_op jit(solution)/shard_map/all_to_all | solution.py:46
  609.5 8.8 %gather_fusion.1 = bf16[1024,1024]{1,0:T(8,128)(2,1)} fusion(bf16[2048,1024]{1,0:T(8,128)(2,1)} %bitcast.18, s32[1024]{0:T(1024)S(1)} %broadcast_clamp_fusion), kind=kCustom, calls=%fused_computation.1 | custom fusion | bytes 4198400 | tf_op jit(solution)/shard_map/jit(_take)/gather | solution.py:53
  618.3 3.1 multiply_reduce_fusion
  621.5 0.8 add_convert_fusion
  622.2 23.0 %all-gather.5.cloned.1.call-done = bf16[128,4096]{1,0:T(8,128)(2,1)} async-done(((bf16[128,1024]{1,0:T(8,128)(2,1)}), bf16[128,4096]{1,0:T(8,128)(2,1)}) %all-gather.5.cloned.1.call-update) | async-done | bytes 1048592 | tf_op jit(solution)/shard_map/all_gather | solution.py:59
  645.3 1.5 fusion.14
  646.8 2.4 convolution_convert_fusion
  (25 shorter events, 0.2 us)
Async XLA Ops:
  7.2 639.7 %copy-start = (bf16[4096,256]{1,0:T(8,128)(2,1)S(1)}, bf16[4096,256]{1,0:T(8,128)(2,1)}, u32[]{:S(2)}) copy-start(bf16[4096,256]{1,0:T(8,128)(2,1)} %param.17) | copy-start | bytes 6291460
  7.2 31.9 %all-gather.3.cloned.1.call-start = ((), (), s32[]{:S(2)}) async-start(), calls=%async_computation.4 | async-start | bytes 1310720 | tf_op jit(solution)/shard_map/all_gather | solution.py:28
  29.6 47.9 %all-to-all-start = ((bf16[32,1,2]{2,1,0:T(2,128)(2,1)}), bf16[32,1,2]{2,1,0:T(2,128)(2,1)S(1)}, u32[]{:S(2)}, u32[]{:S(2)}) async-start(bf16[32,1,2]{2,1,0:T(2,128)(2,1)} %convert_element_type.74), calls=%async_computation | async-start | bytes 32768 | tf_op jit(solution)/shard_map/all_to_all | solution.py:34
  77.5 248.4 %all-to-all-start.1 = ((bf16[32,64,4096]{2,1,0:T(8,128)(2,1)}), bf16[32,64,4096]{2,1,0:T(8,128)(2,1)}, u32[]{:S(2)}, u32[]{:S(2)}) async-start(bf16[32,64,4096]{2,1,0:T(8,128)(2,1)} %bitcast.70), calls=%async_computation.1 | async-start | bytes 33554432 | tf_op jit(solution)/shard_map/all_to_all | solution.py:31
  85.0 459.2 %reduce-scatter.2.cloned.1.call-start = ((), (), s32[]{:S(2)}) async-start(), calls=%async_computation.5 | async-start | bytes 20971520 | tf_op jit(solution)/shard_map/reduce_scatter | solution.py:43
  549.2 7.7 %copy-start.2 = (s32[128,8]{0,1:T(8,128)S(1)}, s32[128,8]{0,1:T(8,128)}, u32[]{:S(2)}) copy-start(s32[128,8]{0,1:T(8,128)} %param.11) | copy-start | bytes 12292
  549.2 7.9 %copy-start.3 = (f32[128,8]{0,1:T(8,128)S(1)}, f32[128,8]{0,1:T(8,128)}, u32[]{:S(2)}) copy-start(f32[128,8]{0,1:T(8,128)} %param.12) | copy-start | bytes 12292
  549.2 60.3 %all-to-all-start.2 = ((bf16[32,64,1024]{2,1,0:T(8,128)(2,1)}), bf16[32,64,1024]{2,1,0:T(8,128)(2,1)}, u32[]{:S(2)}, u32[]{:S(2)}) async-start(bf16[32,64,1024]{2,1,0:T(8,128)(2,1)} %bitcast.71), calls=%async_computation.3 | async-start | bytes 8388608 | tf_op jit(solution)/shard_map/all_to_all | solution.py:46
  556.7 88.6 %all-gather.5.cloned.1.call-start = ((), (), s32[]{:S(2)}) async-start(), calls=%async_computation.6 | async-start | bytes 1310720 | tf_op jit(solution)/shard_map/all_gather | solution.py:59
  609.5 12.0 %copy-start.1 = (bf16[128,1024]{1,0:T(8,128)(2,1)S(1)}, bf16[128,1024]{1,0:T(8,128)(2,1)}, u32[]{:S(2)}) copy-start(bf16[128,1024]{1,0:T(8,128)(2,1)} %param.9) | copy-start | bytes 786436
  618.3 28.5 %copy-start.4 = (f32[4096]{0:T(1024)S(1)}, f32[4096]{0:T(1024)}, u32[]{:S(2)}) copy-start(f32[4096]{0:T(1024)} %param.16) | copy-start | bytes 49156
Sparse Core Ops, SparseCore 0:
  9.7 26.6 all-gather.2
  367.6 176.5 reduce-scatter.1
  622.4 22.8 all-gather.4
where the time goes:
time: 656 us
  waiting for transfers between devices  493 us (75%)
  local copies, waits for them, and re-layouts  55.5 us (8%)
  matrix products  44 us (7%)
  other arithmetic  25.3 us (4%)
  starting transfers between devices  23.6 us (4%)
  between operations  13.9 us (2%)
    all_to_all x1, waiting for transfers between devices, on_device(): lax.all_to_all(empty.at[target].set(picked, mode='drop'), 'ep', split_axi...  241 us
    reduce_scatter x1, waiting for transfers between devices, on_device(): lax.psum_scatter(partial_value.astype(jnp.bfloat16), 'tp', scatter_dimens...  177 us
    all_to_all x1, waiting for transfers between devices, on_device(): lax.all_to_all(reduced.reshape(all_experts * capacity, slice_width), 'ep'...  52.3 us
    dot_general x1, matrix products, on_device(): jnp.einsum('secf,efd->secd', hidden, w_down, preferred_element_type=jnp.f...  26.2 us
    all_gather x1, waiting for transfers between devices, on_device(): lax.all_gather(mixed_out, 'tp', axis=1, tiled=True).astype(jnp.float32)  23 us
    scatter x1, local copies, waits for them, and re-layouts, on_device(): empty.at[target].set(picked, mode='drop')  22 us
    another operation x3, other arithmetic  18.2 us
    gather x1, local copies, waits for them, and re-layouts, on_device(): picked = full_rows[source_row]  16.4 us
  transfers between devices with their start and end apart: 6, of which 4 were waited for; matrix products, arithmetic and copies ran while one was open for 9% of the time, Pallas kernels for 0%

commit v1 on v0

v1 whole, which is shorter than its diff:
```python
import functools

import jax
import jax.numpy as jnp
import numpy as np
from jax import lax
from jax.experimental import pallas as pl
from jax.experimental.pallas import tpu as pltpu
from jax.sharding import Mesh, PartitionSpec as P

AXES = ("y", "z", "c", "x")
SIZES = (4, 4, 2, 4)
LINKS = (("x", 1), ("y", 3), ("z", 1), ("x", 3), ("y", 1), ("z", 3))
STAGES = len(LINKS)
PEERS = 1 << STAGES
HALF = PEERS // 2
BLOCKS = 16
TOK = 128
WIDTH = 1024
SLOTS = 32
CHIP_EXPERTS = 4
PART = (384, 384, 256)
OFFSET = (0, 384, 768)
PARTS = len(PART)


def link_of(part, core, stage):
    return LINKS[(2 * part + core + stage) % STAGES]


def device_number(at):
    return ((at["y"] * 4 + at["z"]) * 2 + at["c"]) * 4 + at["x"]


def all_places():
    for y in range(4):
        for z in range(4):
            for c in range(2):
                for x in range(4):
                    yield dict(y=y, z=z, c=c, x=x)


def stage_pairs(part, stage):
    pairs = []
    for at in all_places():
        axis, mask = link_of(part, at["c"], stage)
        to = dict(at)
        to[axis] ^= mask
        pairs.append((device_number(at), device_number(to)))
    return pairs


def core_pairs():
    return [(device_number(at), device_number(dict(at, c=1 - at["c"]))) for at in all_places()]


def x_pairs(mask):
    return [(device_number(at), device_number(dict(at, x=at["x"] ^ mask))) for at in all_places()]


def place_tables():
    place = np.zeros((128, PARTS, BLOCKS * 4), np.int32)
    owner = np.zeros((128, PARTS, PEERS), np.int32)
    for at in all_places():
        me = device_number(at)
        for part in range(PARTS):
            for j in range(PEERS):
                to = dict(at)
                for stage in range(STAGES):
                    if j >> stage & 1:
                        axis, mask = link_of(part, at["c"], stage)
                        to[axis] ^= mask
                code = (to["y"] * 4 + to["z"]) * 4 + to["x"]
                place[me, part, code] = j
                owner[me, part, j] = code
    return place.reshape(128, -1), owner.reshape(128, -1)


def gather_kernel(place, pick, lo0, hi0, lo1, hi1, lo2, hi2, out, rows, sems):
    block = pl.program_id(0)
    low, high = (lo0, lo1, lo2), (hi0, hi1, hi2)

    def fetch(which, slot, start):
        for x in range(4):
            for part in range(PARTS):
                to = rows.at[slot, :, pl.ds(x * WIDTH + OFFSET[part], PART[part])]
                sem = sems.at[slot, x * PARTS + part]
                if not start:
                    pltpu.make_async_copy(low[part].at[0], to, sem).wait()
                    continue
                j = place[part * PEERS + which * 4 + x]

                @pl.when(j < HALF)
                def _(part=part, j=j, to=to, sem=sem):
                    pltpu.make_async_copy(low[part].at[j], to, sem).start()

                @pl.when(j >= HALF)
                def _(part=part, j=j, to=to, sem=sem):
                    pltpu.make_async_copy(high[part].at[j - HALF], to, sem).start()

    @pl.when(block == 0)
    def _():
        fetch(0, 0, True)

    @pl.when(block + 1 < BLOCKS)
    def _():
        fetch(block + 1, lax.rem(block + 1, 2), True)

    slot = lax.rem(block, 2)
    fetch(block, slot, False)
    for x in range(4):
        cols = slice(x * WIDTH, (x + 1) * WIDTH)
        picked = jnp.dot(pick[0], rows[slot, :, cols], preferred_element_type=jnp.float32)
        picked = picked.astype(jnp.bfloat16)
        for e in range(CHIP_EXPERTS):
            out[e, 0, :, cols] = picked[e * SLOTS : (e + 1) * SLOTS]


def gather_rows(place, pick, pieces):
    flat = [half for pair in pieces for half in pair]
    return pl.pallas_call(
        gather_kernel,
        grid_spec=pltpu.PrefetchScalarGridSpec(
            num_scalar_prefetch=1,
            grid=(BLOCKS,),
            in_specs=[pl.BlockSpec((1, TOK, TOK), lambda b, t: (b, 0, 0))]
            + [pl.BlockSpec(memory_space=pl.ANY)] * 6,
            out_specs=pl.BlockSpec(
                (CHIP_EXPERTS, 1, SLOTS, 4 * WIDTH), lambda b, t: (0, b, 0, 0)
            ),
            scratch_shapes=[
                pltpu.VMEM((2, TOK, 4 * WIDTH), jnp.bfloat16),
                pltpu.SemaphoreType.DMA((2, 4 * PARTS)),
            ],
        ),
        out_shape=jax.ShapeDtypeStruct((CHIP_EXPERTS, BLOCKS, SLOTS, 4 * WIDTH), jnp.bfloat16),
        compiler_params=pltpu.CompilerParams(vmem_limit_bytes=24 << 20),
        cost_estimate=pl.CostEstimate(
            flops=2 * 2048 * 128 * 4096, bytes_accessed=34 << 20, transcendentals=0
        ),
        name="gather_rows",
    )(place, pick, *flat)


def expert_kernel(x, wg, wu, wd, weight, y0, y1, y2, gate, up):
    k = pl.program_id(1)
    g = jnp.dot(x[0], wg[0], preferred_element_type=jnp.float32)
    u = jnp.dot(x[0], wu[0], preferred_element_type=jnp.float32)

    @pl.when(k == 0)
    def _():
        gate[...] = g
        up[...] = u

    @pl.when(k > 0)
    def _():
        gate[...] += g
        up[...] += u

    @pl.when(k == 3)
    def _():
        hidden = (jax.nn.silu(gate[...]) * up[...] * weight[0]).astype(jnp.bfloat16)
        for s in range(4):
            cols = slice(s * WIDTH, (s + 1) * WIDTH)
            y = jnp.dot(hidden, wd[0, :, cols], preferred_element_type=jnp.float32)
            y = y.astype(jnp.bfloat16)
            for part, ref in enumerate((y0, y1, y2)):
                ref[0, s] = y[:, OFFSET[part] : OFFSET[part] + PART[part]]


def run_experts(rows, first, w_gate, w_up, w_down, weight):
    count, ff = w_gate.shape[0], w_gate.shape[2]
    n = BLOCKS * SLOTS
    return pl.pallas_call(
        expert_kernel,
        grid=(count, 4),
        in_specs=[
            pl.BlockSpec((1, n, WIDTH), lambda e, k: (e + first, 0, k)),
            pl.BlockSpec((1, WIDTH, ff), lambda e, k: (e, k, 0)),
            pl.BlockSpec((1, WIDTH, ff), lambda e, k: (e, k, 0)),
            pl.BlockSpec((1, ff, 4 * WIDTH), lambda e, k: (e, 0, 0)),
            pl.BlockSpec((1, n, 1), lambda e, k: (e + first, 0, 0)),
        ],
        out_specs=[pl.BlockSpec((1, 4, n, f), lambda e, k: (e, 0, 0, 0)) for f in PART],
        out_shape=[jax.ShapeDtypeStruct((count, 4, n, f), jnp.bfloat16) for f in PART],
        scratch_shapes=[pltpu.VMEM((n, ff), jnp.float32)] * 2,
        compiler_params=pltpu.CompilerParams(vmem_limit_bytes=48 << 20),
        cost_estimate=pl.CostEstimate(
            flops=2 * 2 * 512 * 4096 * 1152, bytes_accessed=36 << 20, transcendentals=512 * 768
        ),
        name="experts",
    )(rows, w_gate, w_up, w_down, weight)


def scatter_kernel(part, half, step, owner, put, ya, yb, out):
    first = half * HALF + pl.program_id(0) * step
    for i in range(step):
        code = owner[part * PEERS + first + i]
        block, x = lax.div(code, 4), lax.rem(code, 4)
        rows = pl.ds(pl.multiple_of(block * SLOTS, SLOTS), SLOTS)
        y = jnp.concatenate([ya[0, x, rows], ya[1, x, rows], yb[0, x, rows], yb[1, x, rows]], axis=0)
        out[i] = jnp.dot(put[block], y, preferred_element_type=jnp.float32).astype(jnp.bfloat16)


def scatter_rows(part, half, owner, put, ya, yb):
    f, step = PART[part], 8
    whole = pl.BlockSpec(ya.shape, lambda i, t: (0, 0, 0, 0))
    return pl.pallas_call(
        functools.partial(scatter_kernel, part, half, step),
        grid_spec=pltpu.PrefetchScalarGridSpec(
            num_scalar_prefetch=1,
            grid=(HALF // step,),
            in_specs=[pl.BlockSpec(put.shape, lambda i, t: (0, 0, 0)), whole, whole],
            out_specs=pl.BlockSpec((step, TOK, f), lambda i, t: (i, 0, 0)),
        ),
        out_shape=jax.ShapeDtypeStruct((HALF, TOK, f), jnp.bfloat16),
        compiler_params=pltpu.CompilerParams(vmem_limit_bytes=32 << 20),
        cost_estimate=pl.CostEstimate(
            flops=2 * 32 * 128 * 128 * f, bytes_accessed=10 << 20, transcendentals=0
        ),
        name="scatter_rows",
    )(owner, put, ya, yb)


def spread(piece, part):
    held = piece[None]
    for stage in range(STAGES):
        got = lax.ppermute(held, AXES, stage_pairs(part, stage))
        if stage < STAGES - 1:
            held = jnp.concatenate([held, got], axis=0)
    return held, got


def add(a, b):
    return (a.astype(jnp.float32) + b.astype(jnp.float32)).astype(jnp.bfloat16)


def collect(high, low, part):
    for stage in reversed(range(STAGES)):
        got = lax.ppermute(high, AXES, stage_pairs(part, stage))
        if stage:
            cut = 1 << (stage - 1)
            high, low = add(low[cut:], got[cut:]), add(low[:cut], got[:cut])
    return low[0].astype(jnp.float32) + got[0].astype(jnp.float32)


def on_device(
    tokens, keep_mask, expert_ids, route_weight, w_gate, w_up, w_down, norm_gain, kv_weight
):
    y, z, c, x = (lax.axis_index(a) for a in AXES)
    me = ((y * 4 + z) * 2 + c) * 4 + x
    place_all, owner_all = place_tables()
    place = lax.dynamic_index_in_dim(jnp.asarray(place_all), me, 0, keepdims=False)
    owner = lax.dynamic_index_in_dim(jnp.asarray(owner_all), me, 0, keepdims=False)

    experts = 2 * CHIP_EXPERTS * 8
    live = (keep_mask > 0)[:, None, None]
    named = expert_ids[:, :, None] == jnp.arange(experts, dtype=jnp.int32)
    routes = jnp.sum(jnp.where(named & live, route_weight[:, :, None], 0.0), axis=1)
    routes = lax.all_gather(routes, ("y", "z"), axis=0)

    other = [lax.ppermute(w, AXES, core_pairs()) for w in (w_gate, w_up, w_down)]
    pieces = [
        spread(tokens[:, OFFSET[p] : OFFSET[p] + PART[p]], p) for p in range(PARTS)
    ]

    chip = (y * 4 + z) * CHIP_EXPERTS
    mine = [
        lax.dynamic_slice_in_dim(routes, chip + 2 * who, 2, axis=2) for who in (c, 1 - c)
    ]
    mine = jnp.concatenate(mine, axis=2)
    marked = mine > 0
    until = jnp.asarray(np.tril(np.ones((TOK, TOK), np.float32)), jnp.bfloat16)
    rank = jnp.einsum(
        "ts,bse->bet", until, marked.astype(jnp.bfloat16), preferred_element_type=jnp.float32
    )
    rank = jnp.where(marked.transpose(0, 2, 1), rank.astype(jnp.int32) - 1, -1)
    onehot = rank[:, :, None, :] == jnp.arange(SLOTS, dtype=jnp.int32)[None, None, :, None]
    slot_weight = jnp.sum(jnp.where(onehot, mine.transpose(0, 2, 1)[:, :, None, :], 0.0), axis=3)
    slot_weight = slot_weight.transpose(1, 0, 2).reshape(CHIP_EXPERTS, BLOCKS * SLOTS, 1)
    pick = onehot.reshape(BLOCKS, TOK, TOK).astype(jnp.bfloat16)
    put = pick.transpose(0, 2, 1)

    rows = gather_rows(place, pick, pieces).reshape(CHIP_EXPERTS, BLOCKS * SLOTS, 4 * WIDTH)
    ya = run_experts(rows, 0, w_gate, w_up, w_down, slot_weight)
    yb = run_experts(rows, 2, *other, slot_weight)
    high = [scatter_rows(p, 1, owner, put, ya[p], yb[p]) for p in range(PARTS)]
    low = [scatter_rows(p, 0, owner, put, ya[p], yb[p]) for p in range(PARTS)]
    summed = jnp.concatenate([collect(high[p], low[p], p) for p in range(PARTS)], axis=1)
    mixed_out = (tokens.astype(jnp.float32) + summed).astype(jnp.bfloat16)

    full = [mixed_out] + [lax.ppermute(mixed_out, AXES, x_pairs(m)) for m in (1, 2, 3)]
    full = jnp.concatenate(full, axis=1).astype(jnp.float32)
    order = [jnp.bitwise_xor(x, m) * WIDTH for m in range(4)]
    gain = jnp.concatenate([lax.dynamic_slice_in_dim(norm_gain, o, WIDTH) for o in order])
    kv = jnp.concatenate([lax.dynamic_slice_in_dim(kv_weight, o, WIDTH) for o in order])
    mean_square = jnp.mean(full * full, axis=-1, keepdims=True)
    normed = (full * lax.rsqrt(mean_square + 1e-06) * gain).astype(jnp.bfloat16)
    kv_rows = jnp.dot(normed, kv, preferred_element_type=jnp.float32).astype(jnp.bfloat16)
    return (mixed_out, kv_rows)


def solution(mesh):
    fine = Mesh(mesh.devices.reshape(SIZES), AXES)
    ep = ("y", "z", "c")
    in_specs = (
        P(ep, "x"),
        P(ep),
        P(ep, None),
        P(ep, None),
        P(ep, None, "x"),
        P(ep, None, "x"),
        P(ep, "x", None),
        P(),
        P(None, "x"),
    )
    out_specs = (P(ep, "x"), P(ep, "x"))
    return jax.shard_map(
        on_device, mesh=fine, in_specs=in_specs, out_specs=out_specs, check_vma=False
    )
```

time: 656 us -> 385 us (0.59)
  waiting for transfers between devices: 493 us -> 147 us
  Pallas kernels: 0 us -> 77.9 us
  blocking collectives: 0 us -> 56.3 us
  matrix products: 44 us -> 1.26 us
  starting transfers between devices: 23.6 us -> 57.2 us
  local copies, waits for them, and re-layouts: 55.5 us -> 28 us
  between operations: 13.9 us -> 1.22 us
  other arithmetic: 25.3 us -> 14.8 us
    all_to_all x3 -> x0, waiting for transfers between devices: 293 us -> none  [the longest x1 241 us: on_device(): lax.all_to_all(empty.at[target].set(picked, mode='drop'), 'ep', split_axi...]
    reduce_scatter x1 -> x0, waiting for transfers between devices: 177 us -> none  [on_device(): lax.psum_scatter(partial_value.astype(jnp.bfloat16), 'tp', scatter_dimens...]
    ppermute x0 -> x42, waiting for transfers between devices: none -> 147 us  [the longest x18 83.1 us: collect(): got = lax.ppermute(high, AXES, stage_pairs(part, stage))]
    pallas_call x0 -> x9, Pallas kernels: none -> 77.9 us  [the longest x2 45.2 us: run_experts(): pl.pallas_call(expert_kernel, grid=(count, 4), in_specs=[pl.BlockSpec((1,...]
    ppermute x0 -> x42, starting transfers between devices: none -> 57.2 us  [the longest x18 32 us: spread(): got = lax.ppermute(held, AXES, stage_pairs(part, stage))]
    all_gather x0 -> x1, blocking collectives: none -> 56.3 us  [on_device(): routes = lax.all_gather(routes, ('y', 'z'), axis=0)]
    dot_general x3 -> x2, matrix products: 44 us -> 1.26 us  [the longest x1 1.13 us: on_device(): jnp.dot(normed, kv, preferred_element_type=jnp.float32).astype(jnp.bfloat16)]
    gather x2 -> x0, local copies, waits for them, and re-layouts: 25.2 us -> none  [the longest x1 16.4 us: on_device(): picked = full_rows[source_row]]
  transfers between devices with their start and end apart: 6 -> 42, of which waited for: 4 -> 22; matrix products, arithmetic and copies ran while one was open for 9% -> 9% of each run, Pallas kernels for 0% -> 14%
where the time goes in v1:
time: 385 us; the launch traced here: 383 us
  waiting for transfers between devices  147 us (38%)
  Pallas kernels  77.9 us (20%)
  starting transfers between devices  57.2 us (15%)
  blocking collectives  56.3 us (15%)
  local copies, waits for them, and re-layouts  28 us (7%)
  other arithmetic  14.8 us (4%)
    ppermute x18, waiting for transfers between devices, collect(): got = lax.ppermute(high, AXES, stage_pairs(part, stage))  83.1 us
    all_gather x1, blocking collectives, on_device(): routes = lax.all_gather(routes, ('y', 'z'), axis=0)  56.3 us
    ppermute x18, waiting for transfers between devices, spread(): got = lax.ppermute(held, AXES, stage_pairs(part, stage))  55.6 us
    pallas_call x2, Pallas kernels, run_experts(): pl.pallas_call(expert_kernel, grid=(count, 4), in_specs=[pl.BlockSpec((1,...  45.2 us
    ppermute x18, starting transfers between devices, spread(): got = lax.ppermute(held, AXES, stage_pairs(part, stage))  32 us
    pallas_call x1, Pallas kernels, gather_rows(): pl.pallas_call(gather_kernel, grid_spec=pltpu.PrefetchScalarGridSpec(num_...  20.8 us
    ppermute x18, starting transfers between devices, collect(): got = lax.ppermute(high, AXES, stage_pairs(part, stage))  18.9 us
    unnamed x44, local copies, waits for them, and re-layouts  13.6 us
  transfers between devices with their start and end apart: 42, of which 22 were waited for; matrix products, arithmetic and copies ran while one was open for 9% of the time, Pallas kernels for 14%

profile of v1, /device:TPU:0, one launch (start us, length us, event | category | flops | bytes accessed | tf_op | source)
XLA Modules:
  0.0 383.1 jit_solution(7949860564229421967)
XLA Ops:
  1.5 1.7 collective-permute-start.12
  4.1 2.0 collective-permute-start.6
  7.6 1.7 constant_dynamic-update-slice_fusion.15
  9.3 2.4 collective-permute-start.7
  12.6 4.1 %collective-permute-start.13 = (bf16[2,128,256]{2,1,0:T(8,128)(2,1)S(1)}, bf16[2,128,256]{2,1,0:T(8,128)(2,1)S(1)}, u32[]{:S(2)}, u32[]{:S(2)}) collective-permute-start(bf16[2,128,256]{2,1,0:T(8,128)(2,1)S(1)} %pad_maximum_fusion.10), channel_id=1, source_target_pairs={{0,24},{1,25},{2,26},{3,27},{4,5},{5,4},{6,7},{7,6},{8,16},{9,17},... | collective-permute-start | bytes 393224 | tf_op jit(solution)/shard_map/ppermute | solution.py:228
  17.3 2.5 collective-permute-done.13
  20.2 2.9 collective-permute-start.1
  24.7 3.2 collective-permute-start.9
  28.0 2.3 collective-permute-start.15
  32.0 6.4 %collective-permute-done.15 = bf16[8,128,256]{2,1,0:T(8,128)(2,1)S(1)} collective-permute-done((bf16[8,128,256]{2,1,0:T(8,128)(2,1)S(1)}, bf16[8,128,256]{2,1,0:T(8,128)(2,1)S(1)}, u32[]{:S(2)}, u32[]{:S(2)}) %collective-permute-start.15) | collective-permute-done | bytes 524320 | tf_op jit(solution)/shard_map/ppermute | solution.py:228
  43.9 9.5 %collective-permute-done.16 = bf16[16,128,256]{2,1,0:T(8,128)(2,1)S(1)} collective-permute-done((bf16[16,128,256]{2,1,0:T(8,128)(2,1)S(1)}, bf16[16,128,256]{2,1,0:T(8,128)(2,1)S(1)}, u32[]{:S(2)}, u32[]{:S(2)}) %collective-permute-start.16) | collective-permute-done | bytes 1048608 | tf_op jit(solution)/shard_map/ppermute | solution.py:228
  54.5 4.3 %collective-permute-done.3 = bf16[8,128,384]{2,1,0:T(8,128)(2,1)S(1)} collective-permute-done((bf16[8,128,384]{2,1,0:T(8,128)(2,1)S(1)}, bf16[8,128,384]{2,1,0:T(8,128)(2,1)S(1)}, u32[]{:S(2)}, u32[]{:S(2)}) %collective-permute-start.3) | collective-permute-done | bytes 786464 | tf_op jit(solution)/shard_map/ppermute | solution.py:228
  64.5 32.0 %collective-permute-done.4 = bf16[16,128,384]{2,1,0:T(8,128)(2,1)S(1)} collective-permute-done((bf16[16,128,384]{2,1,0:T(8,128)(2,1)S(1)}, bf16[16,128,384]{2,1,0:T(8,128)(2,1)S(1)}, u32[]{:S(2)}, u32[]{:S(2)}) %collective-permute-start.4) | collective-permute-done | bytes 1572896 | tf_op jit(solution)/shard_map/ppermute | solution.py:228
  96.5 1.7 collective-permute-start.11
  100.9 4.7 %collective-permute-start.5 = (bf16[32,128,384]{2,1,0:T(8,128)(2,1)}, bf16[32,128,384]{2,1,0:T(8,128)(2,1)}, u32[]{:S(2)}, u32[]{:S(2)}) collective-permute-start(bf16[32,128,384]{2,1,0:T(8,128)(2,1)} %constant_dynamic-update-slice_fusion.5.lo0), channel_id=1, source_target_pairs={{0,24},{1,25},{2,26},{3,27},{4,5},{5,4},{6,7},{7,6},{8,16},{9,17},... | collective-permute-start | bytes 9437192 | tf_op jit(solution)/shard_map/ppermute | solution.py:228
  105.7 56.3 %all-gather = f32[2048,64]{0,1:T(8,128)S(1)} all-gather(f32[128,64]{0,1:T(8,128)S(1)} %select_reduce_fusion.1), channel_id=2, replica_groups=mesh['y'=4,'z'=4,'c'=2,'x'=4] {'y','z'}, dimensions={0}, use_global_device_ids=true | all-gather | bytes 557056 | tf_op jit(solution)/shard_map/all_gather | solution.py:260
  166.1 2.0 copy.38.pick
  173.6 1.6 copy-done.6
  175.2 20.8 %gather_rows.1 = bf16[4,16,32,4096]{3,2,1,0:T(8,128)(2,1)} custom-call(s32[192]{0:T(256)S(1)} %bitcast.47, bf16[16,128,128]{2,1,0:T(8,128)(2,1)S(1)} %copy-done.4, bf16[32,128,384]{2,1,0:T(8,128)(2,1)} %constant_dynamic-update-slice_fusion.5.lo0, bf16[32,128,384]{2,1,0:T(8,128)(2,1)} %collective-permute-done.5.hi0, ...), custom_call_target="tpu_custom_call" | custom-call | flops 2147483648 | bytes 35651584 | tf_op jit(solution)/shard_map/gather_rows/pallas_call | solution.py:121
  195.9 22.5 %experts.2 = (bf16[2,4,512,384]{3,2,1,0:T(8,128)(2,1)}, bf16[2,4,512,384]{3,2,1,0:T(8,128)(2,1)}, bf16[2,4,512,256]{3,2,1,0:T(8,128)(2,1)S(1)}) custom-call(bf16[4,512,4096]{2,1,0:T(8,128)(2,1)} %bitcast.48, bf16[2,4096,384]{2,1,0:T(8,128)(2,1)} %wg.1, bf16[2,4096,384]{2,1,0:T(8,128)(2,1)} %wu.1, bf16[2,384,4096]{2,1,0:T(8,128)(2,1)} %wd.1, ...), custom_call_target="tpu_custom_call" | custom-call | flops 9663676416 | bytes 37748736 | tf_op jit(solution)/shard_map/experts/pallas_call | solution.py:174
  218.5 22.7 %experts.3 = (bf16[2,4,512,384]{3,2,1,0:T(8,128)(2,1)}, bf16[2,4,512,384]{3,2,1,0:T(8,128)(2,1)}, bf16[2,4,512,256]{3,2,1,0:T(8,128)(2,1)S(1)}) custom-call(bf16[4,512,4096]{2,1,0:T(8,128)(2,1)} %bitcast.49, bf16[2,4096,384]{2,1,0:T(8,128)(2,1)} %collective-permute-done.18.wg, bf16[2,4096,384]{2,1,0:T(8,128)(2,1)} %collective-permute-done.19.wu, ...), custom_call_target="tpu_custom_call" | custom-call | flops 9663676416 | bytes 37748736 | tf_op jit(solution)/shard_map/experts/pallas_call | solution.py:174
  241.2 1.9 copy-done.3
  243.1 2.1 scatter_rows.7
  245.9 2.1 scatter_rows.9
  249.1 1.8 scatter_rows.11
  251.6 1.8 scatter_rows.10
  253.4 34.8 %collective-permute-done.33 = bf16[32,128,256]{2,1,0:T(8,128)(2,1)} collective-permute-done((bf16[32,128,256]{2,1,0:T(8,128)(2,1)S(1)}, bf16[32,128,256]{2,1,0:T(8,128)(2,1)}, u32[]{:S(2)}, u32[]{:S(2)}) %collective-permute-start.33) | collective-permute-done | bytes 2097184 | tf_op jit(solution)/shard_map/ppermute | solution.py:240
  288.2 2.3 add_convert_fusion.5
  291.9 2.1 scatter_rows.6
  294.0 2.1 scatter_rows.8
  296.1 4.6 %collective-permute-done.21 = bf16[32,128,384]{2,1,0:T(8,128)(2,1)} collective-permute-done((bf16[32,128,384]{2,1,0:T(8,128)(2,1)S(1)}, bf16[32,128,384]{2,1,0:T(8,128)(2,1)}, u32[]{:S(2)}, u32[]{:S(2)}) %collective-permute-start.21) | collective-permute-done | bytes 3145760 | tf_op jit(solution)/shard_map/ppermute | solution.py:240
  300.7 3.0 add_convert_fusion.3
  303.8 2.4 collective-permute-done.27
  307.4 3.1 collective-permute-start.28
  311.8 9.5 %collective-permute-done.35 = bf16[8,128,256]{2,1,0:T(8,128)(2,1)S(1)} collective-permute-done((bf16[8,128,256]{2,1,0:T(8,128)(2,1)S(1)}, bf16[8,128,256]{2,1,0:T(8,128)(2,1)S(1)}, u32[]{:S(2)}, u32[]{:S(2)}) %collective-permute-start.35) | collective-permute-done | bytes 524320 | tf_op jit(solution)/shard_map/ppermute | solution.py:240
  321.5 4.8 %collective-permute-done.22 = bf16[16,128,384]{2,1,0:T(8,128)(2,1)S(1)} collective-permute-done((bf16[16,128,384]{2,1,0:T(8,128)(2,1)S(1)}, bf16[16,128,384]{2,1,0:T(8,128)(2,1)S(1)}, u32[]{:S(2)}, u32[]{:S(2)}) %collective-permute-start.22) | collective-permute-done | bytes 1572896 | tf_op jit(solution)/shard_map/ppermute | solution.py:240
  327.7 2.6 collective-permute-done.28
  334.7 10.8 %collective-permute-done.37 = bf16[2,128,256]{2,1,0:T(8,128)(2,1)S(1)} collective-permute-done((bf16[2,128,256]{2,1,0:T(8,128)(2,1)S(1)}, bf16[2,128,256]{2,1,0:T(8,128)(2,1)S(1)}, u32[]{:S(2)}, u32[]{:S(2)}) %collective-permute-start.37) | collective-permute-done | bytes 131104 | tf_op jit(solution)/shard_map/ppermute | solution.py:240
  348.4 2.1 collective-permute-start.30
  350.6 4.3 %collective-permute-done.24 = bf16[4,128,384]{2,1,0:T(8,128)(2,1)S(1)} collective-permute-done((bf16[4,128,384]{2,1,0:T(8,128)(2,1)S(1)}, bf16[4,128,384]{2,1,0:T(8,128)(2,1)S(1)}, u32[]{:S(2)}, u32[]{:S(2)}) %collective-permute-start.24) | collective-permute-done | bytes 393248 | tf_op jit(solution)/shard_map/ppermute | solution.py:240
  355.0 2.1 collective-permute-start.25
  358.4 3.5 collective-permute-done.25
  362.5 1.6 collective-permute-done.31
  366.7 2.1 collective-permute-done.32
  369.1 2.6 collective-permute-start.40
  371.7 2.1 collective-permute-start.41
  375.4 3.5 collective-permute-done.40
  379.0 2.7 collective-permute-done.41
  (151 shorter events, 56.2 us)
Async XLA Ops:
  1.5 11.0 %collective-permute-start.12 = (bf16[1,128,256]{2,1,0:T(8,128)(2,1)S(1)}, bf16[1,128,256]{2,1,0:T(8,128)(2,1)S(1)}, u32[]{:S(2)}, u32[]{:S(2)}) collective-permute-start(bf16[1,128,256]{2,1,0:T(8,128)(2,1)S(1)} %slice_bitcast_fusion.2), channel_id=1, source_target_pairs={{0,32},{1,33},{2,34},{3,35},{4,28},{5,29},{6,30},{7,31},{8,40},{9,... | collective-permute-start | bytes 196616 | tf_op jit(solution)/shard_map/ppermute | solution.py:228
  4.1 5.1 %collective-permute-start.6 = (bf16[1,128,384]{2,1,0:T(8,128)(2,1)S(1)}, bf16[1,128,384]{2,1,0:T(8,128)(2,1)S(1)}, u32[]{:S(2)}, u32[]{:S(2)}) collective-permute-start(bf16[1,128,384]{2,1,0:T(8,128)(2,1)S(1)} %get-tuple-element.62), channel_id=1, source_target_pairs={{0,8},{1,9},{2,10},{3,11},{4,7},{5,6},{6,5},{7,4},{8,0},{9,1},{10,... | collective-permute-start | bytes 294920 | tf_op jit(solution)/shard_map/ppermute | solution.py:228
  6.1 14.1 %collective-permute-start = (bf16[1,128,384]{2,1,0:T(8,128)(2,1)S(1)}, bf16[1,128,384]{2,1,0:T(8,128)(2,1)S(1)}, u32[]{:S(2)}, u32[]{:S(2)}) collective-permute-start(bf16[1,128,384]{2,1,0:T(8,128)(2,1)S(1)} %get-tuple-element.63), channel_id=1, source_target_pairs={{0,1},{1,0},{2,3},{3,2},{4,100},{5,101},{6,102},{7,103},{8,9},{9,8... | collective-permute-start | bytes 294920 | tf_op jit(solution)/shard_map/ppermute | solution.py:228
  9.3 7.4 %collective-permute-start.7 = (bf16[2,128,384]{2,1,0:T(8,128)(2,1)S(1)}, bf16[2,128,384]{2,1,0:T(8,128)(2,1)S(1)}, u32[]{:S(2)}, u32[]{:S(2)}) collective-permute-start(bf16[2,128,384]{2,1,0:T(8,128)(2,1)S(1)} %pad_maximum_fusion.8), channel_id=1, source_target_pairs={{0,3},{1,2},{2,1},{3,0},{4,36},{5,37},{6,38},{7,39},{8,11},{9,10},... | collective-permute-start | bytes 589832 | tf_op jit(solution)/shard_map/ppermute | solution.py:228
  12.6 7.3 %collective-permute-start.13 = (bf16[2,128,256]{2,1,0:T(8,128)(2,1)S(1)}, bf16[2,128,256]{2,1,0:T(8,128)(2,1)S(1)}, u32[]{:S(2)}, u32[]{:S(2)}) collective-permute-start(bf16[2,128,256]{2,1,0:T(8,128)(2,1)S(1)} %pad_maximum_fusion.10), channel_id=1, source_target_pairs={{0,24},{1,25},{2,26},{3,27},{4,5},{5,4},{6,7},{7,6},{8,16},{9,17},... | collective-permute-start | bytes 393224 | tf_op jit(solution)/shard_map/ppermute | solution.py:228
  16.7 7.9 %collective-permute-start.8 = (bf16[4,128,384]{2,1,0:T(8,128)(2,1)S(1)}, bf16[4,128,384]{2,1,0:T(8,128)(2,1)S(1)}, u32[]{:S(2)}, u32[]{:S(2)}) collective-permute-start(bf16[4,128,384]{2,1,0:T(8,128)(2,1)S(1)} %pad_maximum_fusion.5), channel_id=1, source_target_pairs={{0,32},{1,33},{2,34},{3,35},{4,28},{5,29},{6,30},{7,31},{8,40},{9,... | collective-permute-start | bytes 1179656 | tf_op jit(solution)/shard_map/ppermute | solution.py:228
  19.8 8.1 %collective-permute-start.14 = (bf16[4,128,256]{2,1,0:T(8,128)(2,1)S(1)}, bf16[4,128,256]{2,1,0:T(8,128)(2,1)S(1)}, u32[]{:S(2)}, u32[]{:S(2)}) collective-permute-start(bf16[4,128,256]{2,1,0:T(8,128)(2,1)S(1)} %pad_maximum_fusion.6), channel_id=1, source_target_pairs={{0,1},{1,0},{2,3},{3,2},{4,100},{5,101},{6,102},{7,103},{8,9},{9,8... | collective-permute-start | bytes 786440 | tf_op jit(solution)/shard_map/ppermute | solution.py:228
  20.2 10.1 %collective-permute-start.1 = (bf16[2,128,384]{2,1,0:T(8,128)(2,1)S(1)}, bf16[2,128,384]{2,1,0:T(8,128)(2,1)S(1)}, u32[]{:S(2)}, u32[]{:S(2)}) collective-permute-start(bf16[2,128,384]{2,1,0:T(8,128)(2,1)S(1)} %pad_maximum_fusion.7), channel_id=1, source_target_pairs={{0,96},{1,97},{2,98},{3,99},{4,12},{5,13},{6,14},{7,15},{8,104},{9... | collective-permute-start | bytes 589832 | tf_op jit(solution)/shard_map/ppermute | solution.py:228
  24.7 14.0 %collective-permute-start.9 = (bf16[8,128,384]{2,1,0:T(8,128)(2,1)S(1)}, bf16[8,128,384]{2,1,0:T(8,128)(2,1)S(1)}, u32[]{:S(2)}, u32[]{:S(2)}) collective-permute-start(bf16[8,128,384]{2,1,0:T(8,128)(2,1)S(1)} %pad_maximum_fusion.2), channel_id=1, source_target_pairs={{0,24},{1,25},{2,26},{3,27},{4,5},{5,4},{6,7},{7,6},{8,16},{9,17},... | collective-permute-start | bytes 2359304 | tf_op jit(solution)/shard_map/ppermute | solution.py:228
  28.0 10.5 %collective-permute-start.15 = (bf16[8,128,256]{2,1,0:T(8,128)(2,1)S(1)}, bf16[8,128,256]{2,1,0:T(8,128)(2,1)S(1)}, u32[]{:S(2)}, u32[]{:S(2)}) collective-permute-start(bf16[8,128,256]{2,1,0:T(8,128)(2,1)S(1)} %pad_maximum_fusion.3), channel_id=1, source_target_pairs={{0,96},{1,97},{2,98},{3,99},{4,12},{5,13},{6,14},{7,15},{8,104},{9... | collective-permute-start | bytes 1572872 | tf_op jit(solution)/shard_map/ppermute | solution.py:228
  30.3 11.0 %collective-permute-start.2 = (bf16[4,128,384]{2,1,0:T(8,128)(2,1)S(1)}, bf16[4,128,384]{2,1,0:T(8,128)(2,1)S(1)}, u32[]{:S(2)}, u32[]{:S(2)}) collective-permute-start(bf16[4,128,384]{2,1,0:T(8,128)(2,1)S(1)} %pad_maximum_fusion.4), channel_id=1, source_target_pairs={{0,8},{1,9},{2,10},{3,11},{4,7},{5,6},{6,5},{7,4},{8,0},{9,1},{10,... | collective-permute-start | bytes 1179656 | tf_op jit(solution)/shard_map/ppermute | solution.py:228
  38.6 14.9 %collective-permute-start.16 = (bf16[16,128,256]{2,1,0:T(8,128)(2,1)S(1)}, bf16[16,128,256]{2,1,0:T(8,128)(2,1)S(1)}, u32[]{:S(2)}, u32[]{:S(2)}) collective-permute-start(bf16[16,128,256]{2,1,0:T(8,128)(2,1)S(1)} %get-tuple-element.46), channel_id=1, source_target_pairs={{0,8},{1,9},{2,10},{3,11},{4,7},{5,6},{6,5},{7,4},{8,0},{9,1},{10,... | collective-permute-start | bytes 3145736 | tf_op jit(solution)/shard_map/ppermute | solution.py:228
  39.8 22.3 %collective-permute-start.10 = (bf16[16,128,384]{2,1,0:T(8,128)(2,1)S(1)}, bf16[16,128,384]{2,1,0:T(8,128)(2,1)S(1)}, u32[]{:S(2)}, u32[]{:S(2)}) collective-permute-start(bf16[16,128,384]{2,1,0:T(8,128)(2,1)S(1)} %get-tuple-element.40), channel_id=1, source_target_pairs={{0,1},{1,0},{2,3},{3,2},{4,100},{5,101},{6,102},{7,103},{8,9},{9,8... | collective-permute-start | bytes 4718600 | tf_op jit(solution)/shard_map/ppermute | solution.py:228
  41.5 17.3 %collective-permute-start.3 = (bf16[8,128,384]{2,1,0:T(8,128)(2,1)S(1)}, bf16[8,128,384]{2,1,0:T(8,128)(2,1)S(1)}, u32[]{:S(2)}, u32[]{:S(2)}) collective-permute-start(bf16[8,128,384]{2,1,0:T(8,128)(2,1)S(1)} %pad_maximum_fusion.1), channel_id=1, source_target_pairs={{0,3},{1,2},{2,1},{3,0},{4,36},{5,37},{6,38},{7,39},{8,11},{9,10},... | collective-permute-start | bytes 2359304 | tf_op jit(solution)/shard_map/ppermute | solution.py:228
  42.8 175.7 %collective-permute-start.18 = (bf16[2,4096,384]{2,1,0:T(8,128)(2,1)}, bf16[2,4096,384]{2,1,0:T(8,128)(2,1)}, u32[]{:S(2)}, u32[]{:S(2)}) collective-permute-start(bf16[2,4096,384]{2,1,0:T(8,128)(2,1)} %wg.1), channel_id=1, source_target_pairs={{0,4},{1,5},{2,6},{3,7},{4,0},{5,1},{6,2},{7,3},{8,12},{9,13},{10,... | collective-permute-start | bytes 18874376 | tf_op jit(solution)/shard_map/ppermute | solution.py:262
  42.8 175.7 %collective-permute-start.19 = (bf16[2,4096,384]{2,1,0:T(8,128)(2,1)}, bf16[2,4096,384]{2,1,0:T(8,128)(2,1)}, u32[]{:S(2)}, u32[]{:S(2)}) collective-permute-start(bf16[2,4096,384]{2,1,0:T(8,128)(2,1)} %wu.1), channel_id=1, source_target_pairs={{0,4},{1,5},{2,6},{3,7},{4,0},{5,1},{6,2},{7,3},{8,12},{9,13},{10,... | collective-permute-start | bytes 18874376 | tf_op jit(solution)/shard_map/ppermute | solution.py:262
  53.4 165.0 %collective-permute-start.20 = (bf16[2,384,4096]{2,1,0:T(8,128)(2,1)}, bf16[2,384,4096]{2,1,0:T(8,128)(2,1)}, u32[]{:S(2)}, u32[]{:S(2)}) collective-permute-start(bf16[2,384,4096]{2,1,0:T(8,128)(2,1)} %wd.1), channel_id=1, source_target_pairs={{0,4},{1,5},{2,6},{3,7},{4,0},{5,1},{6,2},{7,3},{8,12},{9,13},{10,... | collective-permute-start | bytes 18874376 | tf_op jit(solution)/shard_map/ppermute | solution.py:262
  58.8 40.8 %collective-permute-start.17 = (bf16[32,128,256]{2,1,0:T(8,128)(2,1)S(1)}, bf16[32,128,256]{2,1,0:T(8,128)(2,1)S(1)}, u32[]{:S(2)}, u32[]{:S(2)}) collective-permute-start(bf16[32,128,256]{2,1,0:T(8,128)(2,1)S(1)} %constant_dynamic-update-slice_fusion.27.lo2), channel_id=1, source_target_pairs={{0,3},{1,2},{2,1},{3,0},{4,36},{5,37},{6,38},{7,39},{8,11},{9,10},... | collective-permute-start | bytes 6291464 | tf_op jit(solution)/shard_map/ppermute | solution.py:228
  62.1 34.5 %collective-permute-start.4 = (bf16[16,128,384]{2,1,0:T(8,128)(2,1)S(1)}, bf16[16,128,384]{2,1,0:T(8,128)(2,1)S(1)}, u32[]{:S(2)}, u32[]{:S(2)}) collective-permute-start(bf16[16,128,384]{2,1,0:T(8,128)(2,1)S(1)} %get-tuple-element.42), channel_id=1, source_target_pairs={{0,32},{1,33},{2,34},{3,35},{4,28},{5,29},{6,30},{7,31},{8,40},{9,... | collective-permute-start | bytes 4718600 | tf_op jit(solution)/shard_map/ppermute | solution.py:228
  64.5 41.1 %copy-start.15 = (s32[128]{0:T(128)S(1)}, s32[128]{0:T(128)}, u32[]{:S(2)}) copy-start(s32[128]{0:T(128)} %param.13) | copy-start | bytes 1540
  64.5 41.1 %copy-start.13 = (f32[128,8]{0,1:T(8,128)S(1)}, f32[128,8]{0,1:T(8,128)}, u32[]{:S(2)}) copy-start(f32[128,8]{0,1:T(8,128)} %param.15) | copy-start | bytes 12292
  64.5 41.1 %copy-start.14 = (s32[128,8]{0,1:T(8,128)S(1)}, s32[128,8]{0,1:T(8,128)}, u32[]{:S(2)}) copy-start(s32[128,8]{0,1:T(8,128)} %param.14) | copy-start | bytes 12292
  96.5 76.0 %collective-permute-start.11 = (bf16[32,128,384]{2,1,0:T(8,128)(2,1)}, bf16[32,128,384]{2,1,0:T(8,128)(2,1)}, u32[]{:S(2)}, u32[]{:S(2)}) collective-permute-start(bf16[32,128,384]{2,1,0:T(8,128)(2,1)} %constant_dynamic-update-slice_fusion.16.lo1), channel_id=1, source_target_pairs={{0,96},{1,97},{2,98},{3,99},{4,12},{5,13},{6,14},{7,15},{8,104},{9... | collective-permute-start | bytes 9437192 | tf_op jit(solution)/shard_map/ppermute | solution.py:228
  98.2 63.8 %copy-start.11 = (bf16[128,128,1]{1,0,2:T(8,128)(2,1)S(1)}, bf16[128,128,1]{1,0,2:T(8,128)(2,1)}, u32[]{:S(2)}) copy-start(bf16[128,128,1]{1,0,2:T(8,128)(2,1)} %constant.64) | copy-start | bytes 98308
  100.9 71.7 %collective-permute-start.5 = (bf16[32,128,384]{2,1,0:T(8,128)(2,1)}, bf16[32,128,384]{2,1,0:T(8,128)(2,1)}, u32[]{:S(2)}, u32[]{:S(2)}) collective-permute-start(bf16[32,128,384]{2,1,0:T(8,128)(2,1)} %constant_dynamic-update-slice_fusion.5.lo0), channel_id=1, source_target_pairs={{0,24},{1,25},{2,26},{3,27},{4,5},{5,4},{6,7},{7,6},{8,16},{9,17},... | collective-permute-start | bytes 9437192 | tf_op jit(solution)/shard_map/ppermute | solution.py:228
  218.5 22.7 %copy-start.1 = (bf16[2,4,512,384]{3,2,1,0:T(8,128)(2,1)S(1)}, bf16[2,4,512,384]{3,2,1,0:T(8,128)(2,1)}, u32[]{:S(2)}) copy-start(bf16[2,4,512,384]{3,2,1,0:T(8,128)(2,1)} %get-tuple-element.8.ya) | copy-start | bytes 9437188
  245.2 55.5 %collective-permute-start.21 = (bf16[32,128,384]{2,1,0:T(8,128)(2,1)S(1)}, bf16[32,128,384]{2,1,0:T(8,128)(2,1)}, u32[]{:S(2)}, u32[]{:S(2)}) collective-permute-start(bf16[32,128,384]{2,1,0:T(8,128)(2,1)S(1)} %scatter_rows.7), channel_id=1, source_target_pairs={{0,24},{1,25},{2,26},{3,27},{4,5},{5,4},{6,7},{7,6},{8,16},{9,17},... | collective-permute-start | bytes 9437192 | tf_op jit(solution)/shard_map/ppermute | solution.py:240
  248.0 58.2 %collective-permute-start.27 = (bf16[32,128,384]{2,1,0:T(8,128)(2,1)S(1)}, bf16[32,128,384]{2,1,0:T(8,128)(2,1)S(1)}, u32[]{:S(2)}, u32[]{:S(2)}) collective-permute-start(bf16[32,128,384]{2,1,0:T(8,128)(2,1)S(1)} %scatter_rows.9), channel_id=1, source_target_pairs={{0,96},{1,97},{2,98},{3,99},{4,12},{5,13},{6,14},{7,15},{8,104},{9... | collective-permute-start | bytes 9437192 | tf_op jit(solution)/shard_map/ppermute | solution.py:240
  250.9 37.4 %collective-permute-start.33 = (bf16[32,128,256]{2,1,0:T(8,128)(2,1)S(1)}, bf16[32,128,256]{2,1,0:T(8,128)(2,1)}, u32[]{:S(2)}, u32[]{:S(2)}) collective-permute-start(bf16[32,128,256]{2,1,0:T(8,128)(2,1)S(1)} %scatter_rows.11), channel_id=1, source_target_pairs={{0,3},{1,2},{2,1},{3,0},{4,36},{5,37},{6,38},{7,39},{8,11},{9,10},... | collective-permute-start | bytes 6291464 | tf_op jit(solution)/shard_map/ppermute | solution.py:240
  290.5 19.9 %collective-permute-start.34 = (bf16[16,128,256]{2,1,0:T(8,128)(2,1)S(1)}, bf16[16,128,256]{2,1,0:T(8,128)(2,1)S(1)}, u32[]{:S(2)}, u32[]{:S(2)}) collective-permute-start(bf16[16,128,256]{2,1,0:T(8,128)(2,1)S(1)} %get-tuple-element.19), channel_id=1, source_target_pairs={{0,8},{1,9},{2,10},{3,11},{4,7},{5,6},{6,5},{7,4},{8,0},{9,1},{10,... | collective-permute-start | bytes 3145736 | tf_op jit(solution)/shard_map/ppermute | solution.py:240
  303.7 22.6 %collective-permute-start.22 = (bf16[16,128,384]{2,1,0:T(8,128)(2,1)S(1)}, bf16[16,128,384]{2,1,0:T(8,128)(2,1)S(1)}, u32[]{:S(2)}, u32[]{:S(2)}) collective-permute-start(bf16[16,128,384]{2,1,0:T(8,128)(2,1)S(1)} %get-tuple-element.15), channel_id=1, source_target_pairs={{0,32},{1,33},{2,34},{3,35},{4,28},{5,29},{6,30},{7,31},{8,40},{9,... | collective-permute-start | bytes 4718600 | tf_op jit(solution)/shard_map/ppermute | solution.py:240
  307.4 23.0 %collective-permute-start.28 = (bf16[16,128,384]{2,1,0:T(8,128)(2,1)S(1)}, bf16[16,128,384]{2,1,0:T(8,128)(2,1)S(1)}, u32[]{:S(2)}, u32[]{:S(2)}) collective-permute-start(bf16[16,128,384]{2,1,0:T(8,128)(2,1)S(1)} %get-tuple-element.17), channel_id=1, source_target_pairs={{0,1},{1,0},{2,3},{3,2},{4,100},{5,101},{6,102},{7,103},{8,9},{9,8... | collective-permute-start | bytes 4718600 | tf_op jit(solution)/shard_map/ppermute | solution.py:240
  310.8 10.5 %collective-permute-start.35 = (bf16[8,128,256]{2,1,0:T(8,128)(2,1)S(1)}, bf16[8,128,256]{2,1,0:T(8,128)(2,1)S(1)}, u32[]{:S(2)}, u32[]{:S(2)}) collective-permute-start(bf16[8,128,256]{2,1,0:T(8,128)(2,1)S(1)} %get-tuple-element.29), channel_id=1, source_target_pairs={{0,96},{1,97},{2,98},{3,99},{4,12},{5,13},{6,14},{7,15},{8,104},{9... | collective-permute-start | bytes 1572872 | tf_op jit(solution)/shard_map/ppermute | solution.py:240
  321.4 11.8 %collective-permute-start.36 = (bf16[4,128,256]{2,1,0:T(8,128)(2,1)S(1)}, bf16[4,128,256]{2,1,0:T(8,128)(2,1)S(1)}, u32[]{:S(2)}, u32[]{:S(2)}) collective-permute-start(bf16[4,128,256]{2,1,0:T(8,128)(2,1)S(1)} %get-tuple-element.35), channel_id=1, source_target_pairs={{0,1},{1,0},{2,3},{3,2},{4,100},{5,101},{6,102},{7,103},{8,9},{9,8... | collective-permute-start | bytes 786440 | tf_op jit(solution)/shard_map/ppermute | solution.py:240
  326.8 18.9 %collective-permute-start.23 = (bf16[8,128,384]{2,1,0:T(8,128)(2,1)S(1)}, bf16[8,128,384]{2,1,0:T(8,128)(2,1)}, u32[]{:S(2)}, u32[]{:S(2)}) collective-permute-start(bf16[8,128,384]{2,1,0:T(8,128)(2,1)S(1)} %get-tuple-element.21), channel_id=1, source_target_pairs={{0,3},{1,2},{2,1},{3,0},{4,36},{5,37},{6,38},{7,39},{8,11},{9,10},... | collective-permute-start | bytes 2359304 | tf_op jit(solution)/shard_map/ppermute | solution.py:240
  330.9 16.2 %collective-permute-start.29 = (bf16[8,128,384]{2,1,0:T(8,128)(2,1)S(1)}, bf16[8,128,384]{2,1,0:T(8,128)(2,1)}, u32[]{:S(2)}, u32[]{:S(2)}) collective-permute-start(bf16[8,128,384]{2,1,0:T(8,128)(2,1)S(1)} %get-tuple-element.23), channel_id=1, source_target_pairs={{0,24},{1,25},{2,26},{3,27},{4,5},{5,4},{6,7},{7,6},{8,16},{9,17},... | collective-permute-start | bytes 2359304 | tf_op jit(solution)/shard_map/ppermute | solution.py:240
  333.2 12.3 %collective-permute-start.37 = (bf16[2,128,256]{2,1,0:T(8,128)(2,1)S(1)}, bf16[2,128,256]{2,1,0:T(8,128)(2,1)S(1)}, u32[]{:S(2)}, u32[]{:S(2)}) collective-permute-start(bf16[2,128,256]{2,1,0:T(8,128)(2,1)S(1)} %get-tuple-element.45), channel_id=1, source_target_pairs={{0,24},{1,25},{2,26},{3,27},{4,5},{5,4},{6,7},{7,6},{8,16},{9,17},... | collective-permute-start | bytes 393224 | tf_op jit(solution)/shard_map/ppermute | solution.py:240
  345.6 4.9 %collective-permute-start.38 = (bf16[1,128,256]{2,1,0:T(8,128)(2,1)S(1)}, bf16[1,128,256]{2,1,0:T(8,128)(2,1)S(1)}, u32[]{:S(2)}, u32[]{:S(2)}) collective-permute-start(bf16[1,128,256]{2,1,0:T(8,128)(2,1)S(1)} %add_convert_fusion.28), channel_id=1, source_target_pairs={{0,32},{1,33},{2,34},{3,35},{4,28},{5,29},{6,30},{7,31},{8,40},{9,... | collective-permute-start | bytes 196616 | tf_op jit(solution)/shard_map/ppermute | solution.py:240
  347.0 7.9 %collective-permute-start.24 = (bf16[4,128,384]{2,1,0:T(8,128)(2,1)S(1)}, bf16[4,128,384]{2,1,0:T(8,128)(2,1)S(1)}, u32[]{:S(2)}, u32[]{:S(2)}) collective-permute-start(bf16[4,128,384]{2,1,0:T(8,128)(2,1)S(1)} %get-tuple-element.31), channel_id=1, source_target_pairs={{0,8},{1,9},{2,10},{3,11},{4,7},{5,6},{6,5},{7,4},{8,0},{9,1},{10,... | collective-permute-start | bytes 1179656 | tf_op jit(solution)/shard_map/ppermute | solution.py:240
  348.4 20.5 %copy-start.8 = (bf16[128,1024]{1,0:T(8,128)(2,1)S(1)}, bf16[128,1024]{1,0:T(8,128)(2,1)}, u32[]{:S(2)}) copy-start(bf16[128,1024]{1,0:T(8,128)(2,1)} %param.12) | copy-start | bytes 786436
  348.4 8.6 %collective-permute-start.30 = (bf16[4,128,384]{2,1,0:T(8,128)(2,1)S(1)}, bf16[4,128,384]{2,1,0:T(8,128)(2,1)S(1)}, u32[]{:S(2)}, u32[]{:S(2)}) collective-permute-start(bf16[4,128,384]{2,1,0:T(8,128)(2,1)S(1)} %get-tuple-element.33), channel_id=1, source_target_pairs={{0,32},{1,33},{2,34},{3,35},{4,28},{5,29},{6,30},{7,31},{8,40},{9,... | collective-permute-start | bytes 1179656 | tf_op jit(solution)/shard_map/ppermute | solution.py:240
  355.0 7.0 %collective-permute-start.25 = (bf16[2,128,384]{2,1,0:T(8,128)(2,1)S(1)}, bf16[2,128,384]{2,1,0:T(8,128)(2,1)S(1)}, u32[]{:S(2)}, u32[]{:S(2)}) collective-permute-start(bf16[2,128,384]{2,1,0:T(8,128)(2,1)S(1)} %get-tuple-element.37), channel_id=1, source_target_pairs={{0,96},{1,97},{2,98},{3,99},{4,12},{5,13},{6,14},{7,15},{8,104},{9... | collective-permute-start | bytes 589832 | tf_op jit(solution)/shard_map/ppermute | solution.py:240
  357.2 7.0 %collective-permute-start.31 = (bf16[2,128,384]{2,1,0:T(8,128)(2,1)S(1)}, bf16[2,128,384]{2,1,0:T(8,128)(2,1)S(1)}, u32[]{:S(2)}, u32[]{:S(2)}) collective-permute-start(bf16[2,128,384]{2,1,0:T(8,128)(2,1)S(1)} %get-tuple-element.39), channel_id=1, source_target_pairs={{0,3},{1,2},{2,1},{3,0},{4,36},{5,37},{6,38},{7,39},{8,11},{9,10},... | collective-permute-start | bytes 589832 | tf_op jit(solution)/shard_map/ppermute | solution.py:240
  362.0 4.7 %collective-permute-start.26 = (bf16[1,128,384]{2,1,0:T(8,128)(2,1)S(1)}, bf16[1,128,384]{2,1,0:T(8,128)(2,1)S(1)}, u32[]{:S(2)}, u32[]{:S(2)}) collective-permute-start(bf16[1,128,384]{2,1,0:T(8,128)(2,1)S(1)} %add_convert_fusion.26), channel_id=1, source_target_pairs={{0,1},{1,0},{2,3},{3,2},{4,100},{5,101},{6,102},{7,103},{8,9},{9,8... | collective-permute-start | bytes 294920 | tf_op jit(solution)/shard_map/ppermute | solution.py:240
  364.2 4.7 %collective-permute-start.32 = (bf16[1,128,384]{2,1,0:T(8,128)(2,1)S(1)}, bf16[1,128,384]{2,1,0:T(8,128)(2,1)S(1)}, u32[]{:S(2)}, u32[]{:S(2)}) collective-permute-start(bf16[1,128,384]{2,1,0:T(8,128)(2,1)S(1)} %add_convert_fusion.24), channel_id=1, source_target_pairs={{0,8},{1,9},{2,10},{3,11},{4,7},{5,6},{6,5},{7,4},{8,0},{9,1},{10,... | collective-permute-start | bytes 294920 | tf_op jit(solution)/shard_map/ppermute | solution.py:240
  369.0 6.5 %collective-permute-start.39 = (bf16[128,1024]{1,0:T(8,128)(2,1)S(1)}, bf16[128,1024]{1,0:T(8,128)(2,1)S(1)}, u32[]{:S(2)}, u32[]{:S(2)}) collective-permute-start(bf16[128,1024]{1,0:T(8,128)(2,1)S(1)} %fusion.19), channel_id=1, source_target_pairs={{0,1},{1,0},{2,3},{3,2},{4,5},{5,4},{6,7},{7,6},{8,9},{9,8},{10,11... | collective-permute-start | bytes 786440 | tf_op jit(solution)/shard_map/ppermute | solution.py:292
  369.1 9.9 %collective-permute-start.40 = (bf16[128,1024]{1,0:T(8,128)(2,1)S(1)}, bf16[128,1024]{1,0:T(8,128)(2,1)S(1)}, u32[]{:S(2)}, u32[]{:S(2)}) collective-permute-start(bf16[128,1024]{1,0:T(8,128)(2,1)S(1)} %fusion.19), channel_id=1, source_target_pairs={{0,2},{1,3},{2,0},{3,1},{4,6},{5,7},{6,4},{7,5},{8,10},{9,11},{10,... | collective-permute-start | bytes 786440 | tf_op jit(solution)/shard_map/ppermute | solution.py:292
  371.7 10.0 %collective-permute-start.41 = (bf16[128,1024]{1,0:T(8,128)(2,1)S(1)}, bf16[128,1024]{1,0:T(8,128)(2,1)S(1)}, u32[]{:S(2)}, u32[]{:S(2)}) collective-permute-start(bf16[128,1024]{1,0:T(8,128)(2,1)S(1)} %fusion.19), channel_id=1, source_target_pairs={{0,3},{1,2},{2,1},{3,0},{4,7},{5,6},{6,5},{7,4},{8,11},{9,10},{10,... | collective-permute-start | bytes 786440 | tf_op jit(solution)/shard_map/ppermute | solution.py:292
  (10 other events, 50.9 us)

commit v2 on v1

v2 whole, which is shorter than its diff:
```python
import functools

import jax
import jax.numpy as jnp
import numpy as np
from jax import lax
from jax.experimental import pallas as pl
from jax.experimental.pallas import tpu as pltpu
from jax.sharding import Mesh, PartitionSpec as P

AXES = ("y", "z", "c", "x")
SIZES = (4, 4, 2, 4)
LINKS = (("x", 1), ("y", 3), ("z", 1), ("x", 3), ("y", 1), ("z", 3))
STAGES = len(LINKS)
PEERS = 1 << STAGES
HALF = PEERS // 2
BLOCKS = 16
TOK = 128
WIDTH = 1024
SLOTS = 32
CHIP_EXPERTS = 4
PART = (384, 384, 256)
OFFSET = (0, 384, 768)
PARTS = len(PART)
PAIRS = BLOCKS // 2
GROUPS = 4
SLOT_STEP = SLOTS // GROUPS
GROUP_ROWS = 2 * SLOT_STEP
TILE = PAIRS * GROUP_ROWS
PAIR_ROWS = CHIP_EXPERTS * GROUPS * GROUP_ROWS


def link_of(part, core, stage):
    return LINKS[(2 * part + core + stage) % STAGES]


def device_number(at):
    return ((at["y"] * 4 + at["z"]) * 2 + at["c"]) * 4 + at["x"]


def all_places():
    for y in range(4):
        for z in range(4):
            for c in range(2):
                for x in range(4):
                    yield dict(y=y, z=z, c=c, x=x)


def stage_pairs(part, stage):
    pairs = []
    for at in all_places():
        axis, mask = link_of(part, at["c"], stage)
        to = dict(at)
        to[axis] ^= mask
        pairs.append((device_number(at), device_number(to)))
    return pairs


def core_pairs():
    return [(device_number(at), device_number(dict(at, c=1 - at["c"]))) for at in all_places()]


def x_pairs(mask):
    return [(device_number(at), device_number(dict(at, x=at["x"] ^ mask))) for at in all_places()]


def place_tables():
    place = np.zeros((128, PARTS, BLOCKS * 4), np.int32)
    owner = np.zeros((128, PARTS, PEERS), np.int32)
    for at in all_places():
        me = device_number(at)
        for part in range(PARTS):
            for j in range(PEERS):
                to = dict(at)
                for stage in range(STAGES):
                    if j >> stage & 1:
                        axis, mask = link_of(part, at["c"], stage)
                        to[axis] ^= mask
                code = (to["y"] * 4 + to["z"]) * 4 + to["x"]
                place[me, part, code] = j
                owner[me, part, j] = code
    return place.reshape(128, -1), owner.reshape(128, -1)


def moe_kernel(
    place, groups, pick, weight, lo0, hi0, lo1, hi1, lo2, hi2, g_own, u_own, d_own, g_far, u_far, d_far,
    y0, y1, y2, rows, tok, wide, down, tok_sems, weight_sems, out_sems,
):
    low, high, outs = (lo0, lo1, lo2), (hi0, hi1, hi2), (y0, y1, y2)
    ff = g_own.shape[2]

    def weight_copies(e):
        slot, at = e % 2, e % 2
        gate, up, dn = (g_own, u_own, d_own) if e < 2 else (g_far, u_far, d_far)
        return (
            pltpu.make_async_copy(gate.at[at], wide.at[slot, :, pl.ds(0, ff)], weight_sems.at[slot, 0]),
            pltpu.make_async_copy(up.at[at], wide.at[slot, :, pl.ds(ff, ff)], weight_sems.at[slot, 1]),
            pltpu.make_async_copy(dn.at[at], down.at[slot], weight_sems.at[slot, 2]),
        )

    def fetch(pair, slot, start):
        for blk in range(2):
            for x in range(4):
                for part in range(PARTS):
                    to = tok.at[slot, pl.ds(blk * TOK, TOK), pl.ds(x * WIDTH + OFFSET[part], PART[part])]
                    sem = tok_sems.at[slot, (blk * 4 + x) * PARTS + part]
                    if not start:
                        pltpu.make_async_copy(low[part].at[0], to, sem).wait()
                        continue
                    j = place[part * PEERS + (2 * pair + blk) * 4 + x]

                    @pl.when(j < HALF)
                    def _(part=part, j=j, to=to, sem=sem):
                        pltpu.make_async_copy(low[part].at[j], to, sem).start()

                    @pl.when(j >= HALF)
                    def _(part=part, j=j, to=to, sem=sem):
                        pltpu.make_async_copy(high[part].at[j - HALF], to, sem).start()

    fetch(0, 0, True)
    for copy in weight_copies(0) + weight_copies(1):
        copy.start()

    @pl.loop(0, PAIRS)
    def _(pair):
        slot = lax.rem(pair, 2)

        @pl.when(pair + 1 < PAIRS)
        def _():
            fetch(pair + 1, 1 - slot, True)

        fetch(pair, slot, False)
        at = pl.multiple_of(pair * GROUP_ROWS, GROUP_ROWS)
        for x in range(4):
            cols = slice(x * WIDTH, (x + 1) * WIDTH)
            picked = jnp.dot(pick[pair], tok[slot, :, cols], preferred_element_type=jnp.float32)
            picked = picked.astype(jnp.bfloat16)
            for e in range(CHIP_EXPERTS):
                for g in range(GROUPS):
                    first = (e * GROUPS + g) * GROUP_ROWS
                    rows[e, pl.ds(g * TILE + at, GROUP_ROWS), cols] = picked[first : first + GROUP_ROWS]

    def out_copies(e):
        return [
            pltpu.make_async_copy(
                rows.at[e, :, pl.ds(x * WIDTH + OFFSET[part], PART[part])],
                outs[part].at[e, x],
                out_sems.at[e, x * PARTS + part],
            )
            for x in range(4)
            for part in range(PARTS)
        ]

    for e in range(CHIP_EXPERTS):
        slot = e % 2
        for copy in weight_copies(e):
            copy.wait()

        @pl.loop(0, groups[e])
        def _(g, e=e, slot=slot):
            tile = pl.ds(pl.multiple_of(g * TILE, TILE), TILE)
            both = jnp.dot(rows[e, tile, :], wide[slot], preferred_element_type=jnp.float32)
            hidden = jax.nn.silu(both[:, :ff]) * both[:, ff:] * weight[e, tile]
            hidden = hidden.astype(jnp.bfloat16)
            for x in range(4):
                cols = slice(x * WIDTH, (x + 1) * WIDTH)
                y = jnp.dot(hidden, down[slot, :, cols], preferred_element_type=jnp.float32)
                rows[e, tile, cols] = y.astype(jnp.bfloat16)

        if e + 2 < CHIP_EXPERTS:
            for copy in weight_copies(e + 2):
                copy.start()
        for copy in out_copies(e):
            copy.start()
    for e in range(CHIP_EXPERTS):
        for copy in out_copies(e):
            copy.wait()


def run_experts(place, groups, pick, weight, pieces, own, far):
    flat = [half for pair in pieces for half in pair]
    ff = own[0].shape[2]
    n = BLOCKS * SLOTS
    anywhere = pl.BlockSpec(memory_space=pl.ANY)
    vmem = pl.BlockSpec(memory_space=pltpu.VMEM)
    smem = pl.BlockSpec(memory_space=pltpu.SMEM)
    return pl.pallas_call(
        moe_kernel,
        in_specs=[smem, smem, vmem, vmem] + [anywhere] * 12,
        out_specs=[anywhere] * PARTS,
        out_shape=[jax.ShapeDtypeStruct((CHIP_EXPERTS, 4, n, f), jnp.bfloat16) for f in PART],
        scratch_shapes=[
            pltpu.VMEM((CHIP_EXPERTS, n, 4 * WIDTH), jnp.bfloat16),
            pltpu.VMEM((2, 2 * TOK, 4 * WIDTH), jnp.bfloat16),
            pltpu.VMEM((2, 4 * WIDTH, 2 * ff), jnp.bfloat16),
            pltpu.VMEM((2, ff, 4 * WIDTH), jnp.bfloat16),
            pltpu.SemaphoreType.DMA((2, 8 * PARTS)),
            pltpu.SemaphoreType.DMA((2, 3)),
            pltpu.SemaphoreType.DMA((CHIP_EXPERTS, 4 * PARTS)),
        ],
        compiler_params=pltpu.CompilerParams(vmem_limit_bytes=56 << 20),
        cost_estimate=pl.CostEstimate(
            flops=2 * 2048 * 4096 * 1408, bytes_accessed=72 << 20, transcendentals=2048 * 384
        ),
        name="experts",
    )(place, groups, pick, weight, *flat, *own, *far)


def scatter_kernel(part, half, step, owner, put, y, out):
    first = half * HALF + pl.program_id(0) * step
    for i in range(step):
        code = owner[part * PEERS + first + i]
        block, x = lax.div(code, 4), lax.rem(code, 4)
        at = pl.multiple_of(lax.div(block, 2) * GROUP_ROWS, GROUP_ROWS)
        terms = [
            y[e, x, pl.ds(g * TILE + at, GROUP_ROWS)] for e in range(CHIP_EXPERTS) for g in range(GROUPS)
        ]
        terms = jnp.concatenate(terms, axis=0)
        out[i] = jnp.dot(put[block], terms, preferred_element_type=jnp.float32).astype(jnp.bfloat16)


def scatter_rows(part, half, owner, put, y):
    f, step = PART[part], 8
    return pl.pallas_call(
        functools.partial(scatter_kernel, part, half, step),
        grid_spec=pltpu.PrefetchScalarGridSpec(
            num_scalar_prefetch=1,
            grid=(HALF // step,),
            in_specs=[
                pl.BlockSpec(put.shape, lambda i, t: (0, 0, 0)),
                pl.BlockSpec(y.shape, lambda i, t: (0, 0, 0, 0)),
            ],
            out_specs=pl.BlockSpec((step, TOK, f), lambda i, t: (i, 0, 0)),
        ),
        out_shape=jax.ShapeDtypeStruct((HALF, TOK, f), jnp.bfloat16),
        compiler_params=pltpu.CompilerParams(vmem_limit_bytes=32 << 20),
        cost_estimate=pl.CostEstimate(
            flops=2 * 32 * 128 * 256 * f, bytes_accessed=10 << 20, transcendentals=0
        ),
        name="scatter_rows",
    )(owner, put, y)


def spread(tokens, weights):
    held = [tokens[None, :, OFFSET[p] : OFFSET[p] + PART[p]] for p in range(PARTS)]
    weights, far = list(weights), []
    for stage in range(STAGES):
        if stage != 1 and len(far) < len(weights):
            far.append(lax.ppermute(weights[len(far)], AXES, core_pairs()))
        got = [lax.ppermute(held[p], AXES, stage_pairs(p, stage)) for p in range(PARTS)]
        if stage == STAGES - 1:
            return list(zip(held, got)), far
        held = [jnp.concatenate([h, g], axis=0) for h, g in zip(held, got)]
        if 1 <= stage <= 3:
            held, far, weights = lax.optimization_barrier((held, far, weights))


def add(a, b):
    return (a.astype(jnp.float32) + b.astype(jnp.float32)).astype(jnp.bfloat16)


def collect(high, low, part):
    for stage in reversed(range(STAGES)):
        got = lax.ppermute(high, AXES, stage_pairs(part, stage))
        if stage:
            cut = 1 << (stage - 1)
            high, low = add(low[cut:], got[cut:]), add(low[:cut], got[:cut])
    return low[0].astype(jnp.float32) + got[0].astype(jnp.float32)


def on_device(
    tokens, keep_mask, expert_ids, route_weight, w_gate, w_up, w_down, norm_gain, kv_weight
):
    y, z, c, x = (lax.axis_index(a) for a in AXES)
    me = ((y * 4 + z) * 2 + c) * 4 + x
    place_all, owner_all = place_tables()
    place = lax.dynamic_index_in_dim(jnp.asarray(place_all), me, 0, keepdims=False)
    owner = lax.dynamic_index_in_dim(jnp.asarray(owner_all), me, 0, keepdims=False)

    experts = CHIP_EXPERTS * BLOCKS
    live = (keep_mask > 0)[None, None, :]
    named = expert_ids.T[None] == jnp.arange(experts, dtype=jnp.int32)[:, None, None]
    routes = jnp.sum(jnp.where(named & live, route_weight.T[None], 0.0), axis=1)
    routes = routes.reshape(BLOCKS, CHIP_EXPERTS, TOK)
    routes = lax.all_to_all(routes, ("y", "z"), split_axis=0, concat_axis=0, tiled=True)
    own = (w_gate, w_up, w_down)
    pieces, far = spread(tokens, own)

    mine = jnp.where(c == 0, routes, jnp.concatenate([routes[:, 2:], routes[:, :2]], axis=1))
    marked = mine > 0
    until = jnp.asarray(np.triu(np.ones((TOK, TOK), np.float32)), jnp.bfloat16)
    rank = jnp.einsum(
        "bes,st->bet", marked.astype(jnp.bfloat16), until, preferred_element_type=jnp.float32
    )
    rank = jnp.where(marked, rank.astype(jnp.int32) - 1, -1)
    groups = jnp.max(rank, axis=(0, 2)) // SLOT_STEP + 1
    row = np.arange(GROUPS * GROUP_ROWS)
    row_slot = row // GROUP_ROWS * SLOT_STEP + row % SLOT_STEP
    row_block = row % GROUP_ROWS // SLOT_STEP
    same = jnp.asarray(row_block[:, None] == np.arange(2 * TOK)[None, :] // TOK)

    def by_pair(v):
        v = v.reshape(PAIRS, 2, CHIP_EXPERTS, TOK).transpose(0, 2, 1, 3)
        return v.reshape(PAIRS, CHIP_EXPERTS, 1, 2 * TOK)

    chosen = (by_pair(rank) == jnp.asarray(row_slot, jnp.int32)[:, None]) & same
    slot_weight = jnp.sum(jnp.where(chosen, by_pair(mine), 0.0), axis=3)
    slot_weight = slot_weight.reshape(PAIRS, CHIP_EXPERTS, GROUPS, GROUP_ROWS)
    slot_weight = slot_weight.transpose(1, 2, 0, 3).reshape(CHIP_EXPERTS, BLOCKS * SLOTS, 1)
    pick = chosen.astype(jnp.bfloat16).reshape(PAIRS, PAIR_ROWS, 2 * TOK)
    put = pick.reshape(PAIRS, PAIR_ROWS, 2, TOK).transpose(0, 2, 3, 1)
    put = put.reshape(BLOCKS, TOK, PAIR_ROWS)

    ys = run_experts(place, groups, pick, slot_weight, pieces, own, far)
    high = [scatter_rows(p, 1, owner, put, ys[p]) for p in range(PARTS)]
    low = [scatter_rows(p, 0, owner, put, ys[p]) for p in range(PARTS)]
    summed = jnp.concatenate([collect(high[p], low[p], p) for p in range(PARTS)], axis=1)
    mixed_out = (tokens.astype(jnp.float32) + summed).astype(jnp.bfloat16)

    full = [mixed_out] + [lax.ppermute(mixed_out, AXES, x_pairs(m)) for m in (1, 2, 3)]
    full = jnp.concatenate(full, axis=1).astype(jnp.float32)
    order = [jnp.bitwise_xor(x, m) * WIDTH for m in range(4)]
    gain = jnp.concatenate([lax.dynamic_slice_in_dim(norm_gain, o, WIDTH) for o in order])
    kv = jnp.concatenate([lax.dynamic_slice_in_dim(kv_weight, o, WIDTH) for o in order])
    mean_square = jnp.mean(full * full, axis=-1, keepdims=True)
    normed = (full * lax.rsqrt(mean_square + 1e-06) * gain).astype(jnp.bfloat16)
    kv_rows = jnp.dot(normed, kv, preferred_element_type=jnp.float32).astype(jnp.bfloat16)
    return (mixed_out, kv_rows)


def solution(mesh):
    fine = Mesh(mesh.devices.reshape(SIZES), AXES)
    ep = ("y", "z", "c")
    in_specs = (
        P(ep, "x"),
        P(ep),
        P(ep, None),
        P(ep, None),
        P(ep, None, "x"),
        P(ep, None, "x"),
        P(ep, "x", None),
        P(),
        P(None, "x"),
    )
    out_specs = (P(ep, "x"), P(ep, "x"))
    return jax.shard_map(
        on_device, mesh=fine, in_specs=in_specs, out_specs=out_specs, check_vma=False
    )
```

time: 385 us -> 324 us (0.84)
  blocking collectives: 56.3 us -> 0 us
  starting transfers between devices: 57.2 us -> 91.4 us
  Pallas kernels: 77.9 us -> 52.8 us
  waiting for transfers between devices: 147 us -> 136 us
  local copies, waits for them, and re-layouts: 28 us -> 21.4 us
    all_gather x1 -> x0, blocking collectives: 56.3 us -> none  [on_device(): routes = lax.all_gather(routes, ('y', 'z'), axis=0)]
    ppermute x18, starting transfers between devices: 18.9 us -> 54.5 us  [collect(): got = lax.ppermute(high, AXES, stage_pairs(part, stage))]
    pallas_call x3 -> x1, Pallas kernels: 65.9 us -> 38.2 us  [run_experts(): pl.pallas_call(moe_kernel, in_specs=[smem, smem, vmem, vmem] + [anywhere]...]
    all_to_all x0 -> x1, waiting for transfers between devices: none -> 25.3 us  [on_device(): lax.all_to_all(routes, ('y', 'z'), split_axis=0, concat_axis=0, tiled=True)]
    ppermute x18, waiting for transfers between devices: 83.1 us -> 63.3 us  [collect(): got = lax.ppermute(high, AXES, stage_pairs(part, stage))]
    ppermute x21, waiting for transfers between devices: 55.6 us -> 40 us  [the longest x18 38 us: spread(): lax.ppermute(held[p], AXES, stage_pairs(p, stage))]
    unnamed x44, local copies, waits for them, and re-layouts: 13.6 us -> 7.28 us
    ppermute x21, starting transfers between devices: 33.5 us -> 27.9 us  [the longest x18 26.7 us: spread(): lax.ppermute(held[p], AXES, stage_pairs(p, stage))]
  transfers between devices with their start and end apart: 42 -> 43, of which waited for: 22 -> 25; matrix products, arithmetic and copies ran while one was open for 9% -> 11% of each run, Pallas kernels for 14% -> 3%
where the time goes in v2:
time: 324 us; the launch traced here: 319 us
  waiting for transfers between devices  136 us (42%)
  starting transfers between devices  91.4 us (28%)
  Pallas kernels  52.8 us (16%)
  local copies, waits for them, and re-layouts  21.4 us (7%)
  other arithmetic  15.6 us (5%)
    ppermute x18, waiting for transfers between devices, collect(): got = lax.ppermute(high, AXES, stage_pairs(part, stage))  63.3 us
    ppermute x18, starting transfers between devices, collect(): got = lax.ppermute(high, AXES, stage_pairs(part, stage))  54.5 us
    pallas_call x1, Pallas kernels, run_experts(): pl.pallas_call(moe_kernel, in_specs=[smem, smem, vmem, vmem] + [anywhere]...  38.2 us
    ppermute x18, waiting for transfers between devices, spread(): lax.ppermute(held[p], AXES, stage_pairs(p, stage))  38 us
    ppermute x18, starting transfers between devices, spread(): lax.ppermute(held[p], AXES, stage_pairs(p, stage))  26.7 us
    all_to_all x1, waiting for transfers between devices, on_device(): lax.all_to_all(routes, ('y', 'z'), split_axis=0, concat_axis=0, tiled=True)  25.3 us
    pallas_call x6, Pallas kernels, scatter_rows(): pl.pallas_call(functools.partial(scatter_kernel, part, half, step), grid_...  14.6 us
    convert_element_type x15, other arithmetic, add(): return (a.astype(jnp.float32) + b.astype(jnp.float32)).astype(jnp.bfloat16)  9.36 us
  transfers between devices with their start and end apart: 43, of which 25 were waited for; matrix products, arithmetic and copies ran while one was open for 11% of the time, Pallas kernels for 3%

profile of v2, /device:TPU:0, one launch (start us, length us, event | category | flops | bytes accessed | tf_op | source)
XLA Modules:
  0.0 319.4 jit_solution(8649855162519853917)
XLA Ops:
  5.8 1.9 collective-permute-start.2
  7.7 2.6 collective-permute-start.5
  10.3 2.8 collective-permute-start.1
  13.2 2.8 collective-permute-start.3
  17.4 2.8 collective-permute-done.3
  21.5 5.4 %collective-permute-done.9 = bf16[4,128,256]{2,1,0:T(8,128)(2,1)S(1)} collective-permute-done((bf16[4,128,256]{2,1,0:T(8,128)(2,1)S(1)}, bf16[4,128,256]{2,1,0:T(8,128)(2,1)S(1)}, u32[]{:S(2)}, u32[]{:S(2)}) %collective-permute-start.9) | collective-permute-done | bytes 262176 | tf_op jit(solution)/shard_map/ppermute | solution.py:250
  28.7 2.0 collective-permute-done.10.u_far
  34.8 2.8 collective-permute-start.11
  37.6 5.7 %collective-permute-done.13 = bf16[8,128,256]{2,1,0:T(8,128)(2,1)S(1)} collective-permute-done((bf16[8,128,256]{2,1,0:T(8,128)(2,1)S(1)}, bf16[8,128,256]{2,1,0:T(8,128)(2,1)S(1)}, u32[]{:S(2)}, u32[]{:S(2)}) %collective-permute-start.13) | collective-permute-done | bytes 524320 | tf_op jit(solution)/shard_map/ppermute | solution.py:250
  45.1 2.9 collective-permute-done.11
  51.8 16.9 %collective-permute-done.17 = bf16[16,128,384]{2,1,0:T(8,128)(2,1)S(1)} collective-permute-done((bf16[16,128,384]{2,1,0:T(8,128)(2,1)S(1)}, bf16[16,128,384]{2,1,0:T(8,128)(2,1)S(1)}, u32[]{:S(2)}, u32[]{:S(2)}) %collective-permute-start.17) | collective-permute-done | bytes 1572896 | tf_op jit(solution)/shard_map/ppermute | solution.py:250
  72.8 2.2 collective-permute-start.16
  77.1 2.4 collective-permute-start.20
  80.2 4.2 %all-to-all-start = ((f32[16,4,128]{2,1,0:T(4,128)}), f32[16,4,128]{2,1,0:T(4,128)S(1)}, u32[]{:S(2)}, u32[]{:S(2)}) async-start(f32[16,4,128]{2,1,0:T(4,128)} %bitcast.3), calls=%async_computation | async-start | bytes 65536 | tf_op jit(solution)/shard_map/all_to_all | solution.py:285
  86.7 25.3 %all-to-all-done = f32[16,4,128]{2,1,0:T(4,128)S(1)} async-done(((f32[16,4,128]{2,1,0:T(4,128)}), f32[16,4,128]{2,1,0:T(4,128)S(1)}, u32[]{:S(2)}, u32[]{:S(2)}) %all-to-all-start) | async-done | bytes 32800 | tf_op jit(solution)/shard_map/all_to_all | solution.py:285
  116.3 2.3 eq.55
  122.9 38.2 %experts.1 = (bf16[4,4,512,384]{3,2,1,0:T(8,128)(2,1)}, bf16[4,4,512,384]{3,2,1,0:T(8,128)(2,1)}, bf16[4,4,512,256]{3,2,1,0:T(8,128)(2,1)}) custom-call(s32[192]{0:T(256)} %bitcast.66, s32[4]{0:T(128)} %fusion.26.groups, bf16[8,256,256]{2,1,0:T(8,128)(2,1)} %fusion.12.pick, f32[4,512,1]{2,1,0:T(8,128)} %reshape.69.weight, ...), custom_call_target="tpu_custom_call" | custom-call | flops 23622320128 | bytes 75497472 | tf_op jit(solution)/shard_map/experts/pallas_call | solution.py:187
  161.1 2.8 copy-done.1
  163.9 3.7 %scatter_rows.7 = bf16[32,128,384]{2,1,0:T(8,128)(2,1)} custom-call(s32[192]{0:T(256)S(1)} %bitcast.54, bf16[16,128,256]{2,1,0:T(8,128)(2,1)S(1)} %bitcast.46, bf16[4,4,512,384]{3,2,1,0:T(8,128)(2,1)S(1)} %copy-done.1), custom_call_target="tpu_custom_call" | custom-call | flops 805306368 | bytes 10485760 | tf_op jit(solution)/shard_map/scatter_rows/pallas_call | solution.py:224
  167.6 6.6 %collective-permute-start.21 = (bf16[32,128,384]{2,1,0:T(8,128)(2,1)}, bf16[32,128,384]{2,1,0:T(8,128)(2,1)}, u32[]{:S(2)}, u32[]{:S(2)}) collective-permute-start(bf16[32,128,384]{2,1,0:T(8,128)(2,1)} %scatter_rows.7), channel_id=1, source_target_pairs={{0,24},{1,25},{2,26},{3,27},{4,5},{5,4},{6,7},{7,6},{8,16},{9,17},... | collective-permute-start | bytes 9437192 | tf_op jit(solution)/shard_map/ppermute | solution.py:264
  174.3 2.4 scatter_rows.9
  176.6 1.9 collective-permute-start.27
  178.6 1.9 scatter_rows.11
  180.5 2.9 collective-permute-start.33
  183.4 1.9 scatter_rows.10
  185.3 2.4 scatter_rows.6
  187.7 21.6 %collective-permute-done.33 = bf16[32,128,256]{2,1,0:T(8,128)(2,1)S(1)} collective-permute-done((bf16[32,128,256]{2,1,0:T(8,128)(2,1)S(1)}, bf16[32,128,256]{2,1,0:T(8,128)(2,1)S(1)}, u32[]{:S(2)}, u32[]{:S(2)}) %collective-permute-start.33) | collective-permute-done | bytes 2097184 | tf_op jit(solution)/shard_map/ppermute | solution.py:264
  210.0 5.8 %collective-permute-start.34 = (bf16[16,128,256]{2,1,0:T(8,128)(2,1)S(1)}, bf16[16,128,256]{2,1,0:T(8,128)(2,1)S(1)}, u32[]{:S(2)}, u32[]{:S(2)}) collective-permute-start(bf16[16,128,256]{2,1,0:T(8,128)(2,1)S(1)} %get-tuple-element.49), channel_id=1, source_target_pairs={{0,8},{1,9},{2,10},{3,11},{4,7},{5,6},{6,5},{7,4},{8,0},{9,1},{10,... | collective-permute-start | bytes 3145736 | tf_op jit(solution)/shard_map/ppermute | solution.py:264
  215.8 2.3 scatter_rows.8
  218.1 3.2 add_convert_fusion.3
  221.3 5.8 %collective-permute-start.22 = (bf16[16,128,384]{2,1,0:T(8,128)(2,1)S(1)}, bf16[16,128,384]{2,1,0:T(8,128)(2,1)S(1)}, u32[]{:S(2)}, u32[]{:S(2)}) collective-permute-start(bf16[16,128,384]{2,1,0:T(8,128)(2,1)S(1)} %get-tuple-element.45), channel_id=1, source_target_pairs={{0,32},{1,33},{2,34},{3,35},{4,28},{5,29},{6,30},{7,31},{8,40},{9,... | collective-permute-start | bytes 4718600 | tf_op jit(solution)/shard_map/ppermute | solution.py:264
  228.3 5.6 %collective-permute-done.34 = bf16[16,128,256]{2,1,0:T(8,128)(2,1)S(1)} collective-permute-done((bf16[16,128,256]{2,1,0:T(8,128)(2,1)S(1)}, bf16[16,128,256]{2,1,0:T(8,128)(2,1)S(1)}, u32[]{:S(2)}, u32[]{:S(2)}) %collective-permute-start.34) | collective-permute-done | bytes 1048608 | tf_op jit(solution)/shard_map/ppermute | solution.py:264
  234.2 5.7 %collective-permute-start.35 = (bf16[8,128,256]{2,1,0:T(8,128)(2,1)S(1)}, bf16[8,128,256]{2,1,0:T(8,128)(2,1)S(1)}, u32[]{:S(2)}, u32[]{:S(2)}) collective-permute-start(bf16[8,128,256]{2,1,0:T(8,128)(2,1)S(1)} %get-tuple-element.59), channel_id=1, source_target_pairs={{0,96},{1,97},{2,98},{3,99},{4,12},{5,13},{6,14},{7,15},{8,104},{9... | collective-permute-start | bytes 1572872 | tf_op jit(solution)/shard_map/ppermute | solution.py:264
  239.9 7.2 %collective-permute-done.35 = bf16[8,128,256]{2,1,0:T(8,128)(2,1)S(1)} collective-permute-done((bf16[8,128,256]{2,1,0:T(8,128)(2,1)S(1)}, bf16[8,128,256]{2,1,0:T(8,128)(2,1)S(1)}, u32[]{:S(2)}, u32[]{:S(2)}) %collective-permute-start.35) | collective-permute-done | bytes 524320 | tf_op jit(solution)/shard_map/ppermute | solution.py:264
  247.3 2.5 collective-permute-done.22
  250.3 3.8 %collective-permute-start.23 = (bf16[8,128,384]{2,1,0:T(8,128)(2,1)S(1)}, bf16[8,128,384]{2,1,0:T(8,128)(2,1)}, u32[]{:S(2)}, u32[]{:S(2)}) collective-permute-start(bf16[8,128,384]{2,1,0:T(8,128)(2,1)S(1)} %get-tuple-element.51), channel_id=1, source_target_pairs={{0,3},{1,2},{2,1},{3,0},{4,36},{5,37},{6,38},{7,39},{8,11},{9,10},... | collective-permute-start | bytes 2359304 | tf_op jit(solution)/shard_map/ppermute | solution.py:264
  256.3 3.5 %collective-permute-done.36 = bf16[4,128,256]{2,1,0:T(8,128)(2,1)S(1)} collective-permute-done((bf16[4,128,256]{2,1,0:T(8,128)(2,1)S(1)}, bf16[4,128,256]{2,1,0:T(8,128)(2,1)S(1)}, u32[]{:S(2)}, u32[]{:S(2)}) %collective-permute-start.36) | collective-permute-done | bytes 262176 | tf_op jit(solution)/shard_map/ppermute | solution.py:264
  261.5 8.6 %collective-permute-done.37 = bf16[2,128,256]{2,1,0:T(8,128)(2,1)S(1)} collective-permute-done((bf16[2,128,256]{2,1,0:T(8,128)(2,1)S(1)}, bf16[2,128,256]{2,1,0:T(8,128)(2,1)S(1)}, u32[]{:S(2)}, u32[]{:S(2)}) %collective-permute-start.37) | collective-permute-done | bytes 131104 | tf_op jit(solution)/shard_map/ppermute | solution.py:264
  270.1 2.7 collective-permute-start.38
  274.1 4.9 %collective-permute-start.24 = (bf16[4,128,384]{2,1,0:T(8,128)(2,1)S(1)}, bf16[4,128,384]{2,1,0:T(8,128)(2,1)S(1)}, u32[]{:S(2)}, u32[]{:S(2)}) collective-permute-start(bf16[4,128,384]{2,1,0:T(8,128)(2,1)S(1)} %get-tuple-element.61), channel_id=1, source_target_pairs={{0,8},{1,9},{2,10},{3,11},{4,7},{5,6},{6,5},{7,4},{8,0},{9,1},{10,... | collective-permute-start | bytes 1179656 | tf_op jit(solution)/shard_map/ppermute | solution.py:264
  280.5 4.3 %collective-permute-done.24 = bf16[4,128,384]{2,1,0:T(8,128)(2,1)S(1)} collective-permute-done((bf16[4,128,384]{2,1,0:T(8,128)(2,1)S(1)}, bf16[4,128,384]{2,1,0:T(8,128)(2,1)S(1)}, u32[]{:S(2)}, u32[]{:S(2)}) %collective-permute-start.24) | collective-permute-done | bytes 393248 | tf_op jit(solution)/shard_map/ppermute | solution.py:264
  284.9 5.5 %collective-permute-start.25 = (bf16[2,128,384]{2,1,0:T(8,128)(2,1)S(1)}, bf16[2,128,384]{2,1,0:T(8,128)(2,1)S(1)}, u32[]{:S(2)}, u32[]{:S(2)}) collective-permute-start(bf16[2,128,384]{2,1,0:T(8,128)(2,1)S(1)} %get-tuple-element.67), channel_id=1, source_target_pairs={{0,96},{1,97},{2,98},{3,99},{4,12},{5,13},{6,14},{7,15},{8,104},{9... | collective-permute-start | bytes 589832 | tf_op jit(solution)/shard_map/ppermute | solution.py:264
  294.1 5.7 %collective-permute-done.31 = bf16[2,128,384]{2,1,0:T(8,128)(2,1)S(1)} collective-permute-done((bf16[2,128,384]{2,1,0:T(8,128)(2,1)S(1)}, bf16[2,128,384]{2,1,0:T(8,128)(2,1)S(1)}, u32[]{:S(2)}, u32[]{:S(2)}) %collective-permute-start.31) | collective-permute-done | bytes 196640 | tf_op jit(solution)/shard_map/ppermute | solution.py:264
  299.8 3.6 %collective-permute-start.32 = (bf16[1,128,384]{2,1,0:T(8,128)(2,1)S(1)}, bf16[1,128,384]{2,1,0:T(8,128)(2,1)S(1)}, u32[]{:S(2)}, u32[]{:S(2)}) collective-permute-start(bf16[1,128,384]{2,1,0:T(8,128)(2,1)S(1)} %add_convert_fusion.24), channel_id=1, source_target_pairs={{0,8},{1,9},{2,10},{3,11},{4,7},{5,6},{6,5},{7,4},{8,0},{9,1},{10,... | collective-permute-start | bytes 294920 | tf_op jit(solution)/shard_map/ppermute | solution.py:264
  303.5 2.5 collective-permute-done.32
  308.0 3.0 collective-permute-start.41
  312.6 2.6 collective-permute-done.40
  315.3 2.7 collective-permute-done.41
  (158 shorter events, 55.5 us)
Async XLA Ops:
  0.6 19.6 %collective-permute-start.6 = (bf16[2,4096,384]{2,1,0:T(8,128)(2,1)}, bf16[2,4096,384]{2,1,0:T(8,128)(2,1)S(1)}, u32[]{:S(2)}, u32[]{:S(2)}) collective-permute-start(bf16[2,4096,384]{2,1,0:T(8,128)(2,1)} %g_own.1), channel_id=1, source_target_pairs={{0,4},{1,5},{2,6},{3,7},{4,0},{5,1},{6,2},{7,3},{8,12},{9,13},{10,... | collective-permute-start | bytes 18874376 | tf_op jit(solution)/shard_map/ppermute | solution.py:249
  1.6 6.1 %collective-permute-start.4 = (bf16[1,128,256]{2,1,0:T(8,128)(2,1)S(1)}, bf16[1,128,256]{2,1,0:T(8,128)(2,1)S(1)}, u32[]{:S(2)}, u32[]{:S(2)}) collective-permute-start(bf16[1,128,256]{2,1,0:T(8,128)(2,1)S(1)} %slice_bitcast_fusion.2), channel_id=1, source_target_pairs={{0,32},{1,33},{2,34},{3,35},{4,28},{5,29},{6,30},{7,31},{8,40},{9,... | collective-permute-start | bytes 196616 | tf_op jit(solution)/shard_map/ppermute | solution.py:250
  4.2 6.1 %collective-permute-start = (bf16[1,128,384]{2,1,0:T(8,128)(2,1)S(1)}, bf16[1,128,384]{2,1,0:T(8,128)(2,1)S(1)}, u32[]{:S(2)}, u32[]{:S(2)}) collective-permute-start(bf16[1,128,384]{2,1,0:T(8,128)(2,1)S(1)} %get-tuple-element.73), channel_id=1, source_target_pairs={{0,1},{1,0},{2,3},{3,2},{4,100},{5,101},{6,102},{7,103},{8,9},{9,8... | collective-permute-start | bytes 294920 | tf_op jit(solution)/shard_map/ppermute | solution.py:250
  5.8 7.4 %collective-permute-start.2 = (bf16[1,128,384]{2,1,0:T(8,128)(2,1)S(1)}, bf16[1,128,384]{2,1,0:T(8,128)(2,1)S(1)}, u32[]{:S(2)}, u32[]{:S(2)}) collective-permute-start(bf16[1,128,384]{2,1,0:T(8,128)(2,1)S(1)} %get-tuple-element.72), channel_id=1, source_target_pairs={{0,8},{1,9},{2,10},{3,11},{4,7},{5,6},{6,5},{7,4},{8,0},{9,1},{10,... | collective-permute-start | bytes 294920 | tf_op jit(solution)/shard_map/ppermute | solution.py:250
  7.7 8.4 %collective-permute-start.5 = (bf16[2,128,256]{2,1,0:T(8,128)(2,1)S(1)}, bf16[2,128,256]{2,1,0:T(8,128)(2,1)S(1)}, u32[]{:S(2)}, u32[]{:S(2)}) collective-permute-start(bf16[2,128,256]{2,1,0:T(8,128)(2,1)S(1)} %pad_maximum_fusion.13), channel_id=1, source_target_pairs={{0,24},{1,25},{2,26},{3,27},{4,5},{5,4},{6,7},{7,6},{8,16},{9,17},... | collective-permute-start | bytes 393224 | tf_op jit(solution)/shard_map/ppermute | solution.py:250
  10.3 7.0 %collective-permute-start.1 = (bf16[2,128,384]{2,1,0:T(8,128)(2,1)S(1)}, bf16[2,128,384]{2,1,0:T(8,128)(2,1)S(1)}, u32[]{:S(2)}, u32[]{:S(2)}) collective-permute-start(bf16[2,128,384]{2,1,0:T(8,128)(2,1)S(1)} %pad_maximum_fusion.10), channel_id=1, source_target_pairs={{0,96},{1,97},{2,98},{3,99},{4,12},{5,13},{6,14},{7,15},{8,104},{9... | collective-permute-start | bytes 589832 | tf_op jit(solution)/shard_map/ppermute | solution.py:250
  13.2 7.0 %collective-permute-start.3 = (bf16[2,128,384]{2,1,0:T(8,128)(2,1)S(1)}, bf16[2,128,384]{2,1,0:T(8,128)(2,1)S(1)}, u32[]{:S(2)}, u32[]{:S(2)}) collective-permute-start(bf16[2,128,384]{2,1,0:T(8,128)(2,1)S(1)} %pad_maximum_fusion.11), channel_id=1, source_target_pairs={{0,3},{1,2},{2,1},{3,0},{4,36},{5,37},{6,38},{7,39},{8,11},{9,10},... | collective-permute-start | bytes 589832 | tf_op jit(solution)/shard_map/ppermute | solution.py:250
  20.2 27.9 %copy-start.13 = (bf16[2,4096,384]{2,1,0:T(8,128)(2,1)}, bf16[2,4096,384]{2,1,0:T(8,128)(2,1)S(1)}, u32[]{:S(2)}) copy-start(bf16[2,4096,384]{2,1,0:T(8,128)(2,1)S(1)} %collective-permute-done.6.g_far) | copy-start | bytes 18874372
  20.3 10.4 %collective-permute-start.10 = (bf16[2,4096,384]{2,1,0:T(8,128)(2,1)}, bf16[2,4096,384]{2,1,0:T(8,128)(2,1)S(1)}, u32[]{:S(2)}, u32[]{:S(2)}) collective-permute-start(bf16[2,4096,384]{2,1,0:T(8,128)(2,1)} %u_own.1), channel_id=1, source_target_pairs={{0,4},{1,5},{2,6},{3,7},{4,0},{5,1},{6,2},{7,3},{8,12},{9,13},{10,... | collective-permute-start | bytes 18874376 | tf_op jit(solution)/shard_map/ppermute | solution.py:249
  20.3 7.9 %collective-permute-start.8 = (bf16[4,128,384]{2,1,0:T(8,128)(2,1)S(1)}, bf16[4,128,384]{2,1,0:T(8,128)(2,1)S(1)}, u32[]{:S(2)}, u32[]{:S(2)}) collective-permute-start(bf16[4,128,384]{2,1,0:T(8,128)(2,1)S(1)} %pad_maximum_fusion.8), channel_id=1, source_target_pairs={{0,32},{1,33},{2,34},{3,35},{4,28},{5,29},{6,30},{7,31},{8,40},{9,... | collective-permute-start | bytes 1179656 | tf_op jit(solution)/shard_map/ppermute | solution.py:250
  20.6 6.4 %collective-permute-start.9 = (bf16[4,128,256]{2,1,0:T(8,128)(2,1)S(1)}, bf16[4,128,256]{2,1,0:T(8,128)(2,1)S(1)}, u32[]{:S(2)}, u32[]{:S(2)}) collective-permute-start(bf16[4,128,256]{2,1,0:T(8,128)(2,1)S(1)} %pad_maximum_fusion.9), channel_id=1, source_target_pairs={{0,1},{1,0},{2,3},{3,2},{4,100},{5,101},{6,102},{7,103},{8,9},{9,8... | collective-permute-start | bytes 786440 | tf_op jit(solution)/shard_map/ppermute | solution.py:250
  20.8 7.8 %collective-permute-start.7 = (bf16[4,128,384]{2,1,0:T(8,128)(2,1)S(1)}, bf16[4,128,384]{2,1,0:T(8,128)(2,1)S(1)}, u32[]{:S(2)}, u32[]{:S(2)}) collective-permute-start(bf16[4,128,384]{2,1,0:T(8,128)(2,1)S(1)} %pad_maximum_fusion.7), channel_id=1, source_target_pairs={{0,8},{1,9},{2,10},{3,11},{4,7},{5,6},{6,5},{7,4},{8,0},{9,1},{10,... | collective-permute-start | bytes 1179656 | tf_op jit(solution)/shard_map/ppermute | solution.py:250
  30.7 17.5 %collective-permute-start.14 = (bf16[2,384,4096]{2,1,0:T(8,128)(2,1)S(1)}, bf16[2,384,4096]{2,1,0:T(8,128)(2,1)S(1)}, u32[]{:S(2)}, u32[]{:S(2)}) collective-permute-start(bf16[2,384,4096]{2,1,0:T(8,128)(2,1)S(1)} %copy-done.12), channel_id=1, source_target_pairs={{0,4},{1,5},{2,6},{3,7},{4,0},{5,1},{6,2},{7,3},{8,12},{9,13},{10,... | collective-permute-start | bytes 18874376 | tf_op jit(solution)/shard_map/ppermute | solution.py:249
  31.7 13.2 %collective-permute-start.12 = (bf16[8,128,384]{2,1,0:T(8,128)(2,1)S(1)}, bf16[8,128,384]{2,1,0:T(8,128)(2,1)S(1)}, u32[]{:S(2)}, u32[]{:S(2)}) collective-permute-start(bf16[8,128,384]{2,1,0:T(8,128)(2,1)S(1)} %pad_maximum_fusion.5), channel_id=1, source_target_pairs={{0,24},{1,25},{2,26},{3,27},{4,5},{5,4},{6,7},{7,6},{8,16},{9,17},... | collective-permute-start | bytes 2359304 | tf_op jit(solution)/shard_map/ppermute | solution.py:250
  32.9 10.4 %collective-permute-start.13 = (bf16[8,128,256]{2,1,0:T(8,128)(2,1)S(1)}, bf16[8,128,256]{2,1,0:T(8,128)(2,1)S(1)}, u32[]{:S(2)}, u32[]{:S(2)}) collective-permute-start(bf16[8,128,256]{2,1,0:T(8,128)(2,1)S(1)} %pad_maximum_fusion.6), channel_id=1, source_target_pairs={{0,96},{1,97},{2,98},{3,99},{4,12},{5,13},{6,14},{7,15},{8,104},{9... | collective-permute-start | bytes 1572872 | tf_op jit(solution)/shard_map/ppermute | solution.py:250
  34.8 13.2 %collective-permute-start.11 = (bf16[8,128,384]{2,1,0:T(8,128)(2,1)S(1)}, bf16[8,128,384]{2,1,0:T(8,128)(2,1)S(1)}, u32[]{:S(2)}, u32[]{:S(2)}) collective-permute-start(bf16[8,128,384]{2,1,0:T(8,128)(2,1)S(1)} %pad_maximum_fusion.4), channel_id=1, source_target_pairs={{0,3},{1,2},{2,1},{3,0},{4,36},{5,37},{6,38},{7,39},{8,11},{9,10},... | collective-permute-start | bytes 2359304 | tf_op jit(solution)/shard_map/ppermute | solution.py:250
  48.2 24.5 %copy-start.15 = (bf16[2,384,4096]{2,1,0:T(8,128)(2,1)}, bf16[2,384,4096]{2,1,0:T(8,128)(2,1)S(1)}, u32[]{:S(2)}) copy-start(bf16[2,384,4096]{2,1,0:T(8,128)(2,1)S(1)} %collective-permute-done.14.d_far) | copy-start | bytes 18874372
  48.2 20.5 %collective-permute-start.17 = (bf16[16,128,384]{2,1,0:T(8,128)(2,1)S(1)}, bf16[16,128,384]{2,1,0:T(8,128)(2,1)S(1)}, u32[]{:S(2)}, u32[]{:S(2)}) collective-permute-start(bf16[16,128,384]{2,1,0:T(8,128)(2,1)S(1)} %pad_maximum_fusion.1), channel_id=1, source_target_pairs={{0,1},{1,0},{2,3},{3,2},{4,100},{5,101},{6,102},{7,103},{8,9},{9,8... | collective-permute-start | bytes 4718600 | tf_op jit(solution)/shard_map/ppermute | solution.py:250
  48.3 23.1 %collective-permute-start.15 = (bf16[16,128,384]{2,1,0:T(8,128)(2,1)S(1)}, bf16[16,128,384]{2,1,0:T(8,128)(2,1)S(1)}, u32[]{:S(2)}, u32[]{:S(2)}) collective-permute-start(bf16[16,128,384]{2,1,0:T(8,128)(2,1)S(1)} %pad_maximum_fusion), channel_id=1, source_target_pairs={{0,32},{1,33},{2,34},{3,35},{4,28},{5,29},{6,30},{7,31},{8,40},{9,... | collective-permute-start | bytes 4718600 | tf_op jit(solution)/shard_map/ppermute | solution.py:250
  48.5 27.5 %collective-permute-start.19 = (bf16[16,128,256]{2,1,0:T(8,128)(2,1)S(1)}, bf16[16,128,256]{2,1,0:T(8,128)(2,1)S(1)}, u32[]{:S(2)}, u32[]{:S(2)}) collective-permute-start(bf16[16,128,256]{2,1,0:T(8,128)(2,1)S(1)} %pad_maximum_fusion.2), channel_id=1, source_target_pairs={{0,8},{1,9},{2,10},{3,11},{4,7},{5,6},{6,5},{7,4},{8,0},{9,1},{10,... | collective-permute-start | bytes 3145736 | tf_op jit(solution)/shard_map/ppermute | solution.py:250
  70.1 52.8 %collective-permute-start.18 = (bf16[32,128,384]{2,1,0:T(8,128)(2,1)}, bf16[32,128,384]{2,1,0:T(8,128)(2,1)}, u32[]{:S(2)}, u32[]{:S(2)}) collective-permute-start(bf16[32,128,384]{2,1,0:T(8,128)(2,1)} %constant_dynamic-update-slice_fusion.2.lo1), channel_id=1, source_target_pairs={{0,96},{1,97},{2,98},{3,99},{4,12},{5,13},{6,14},{7,15},{8,104},{9... | collective-permute-start | bytes 9437192 | tf_op jit(solution)/shard_map/ppermute | solution.py:250
  72.7 39.3 %copy-start.6 = (bf16[128,128,1]{1,0,2:T(8,128)(2,1)S(1)}, bf16[128,128,1]{1,0,2:T(8,128)(2,1)}, u32[]{:S(2)}) copy-start(bf16[128,128,1]{1,0,2:T(8,128)(2,1)} %constant.83) | copy-start | bytes 98308
  72.8 50.2 %collective-permute-start.16 = (bf16[32,128,384]{2,1,0:T(8,128)(2,1)}, bf16[32,128,384]{2,1,0:T(8,128)(2,1)}, u32[]{:S(2)}, u32[]{:S(2)}) collective-permute-start(bf16[32,128,384]{2,1,0:T(8,128)(2,1)} %constant_dynamic-update-slice_fusion.lo0), channel_id=1, source_target_pairs={{0,24},{1,25},{2,26},{3,27},{4,5},{5,4},{6,7},{7,6},{8,16},{9,17},... | collective-permute-start | bytes 9437192 | tf_op jit(solution)/shard_map/ppermute | solution.py:250
  77.1 45.8 %collective-permute-start.20 = (bf16[32,128,256]{2,1,0:T(8,128)(2,1)}, bf16[32,128,256]{2,1,0:T(8,128)(2,1)}, u32[]{:S(2)}, u32[]{:S(2)}) collective-permute-start(bf16[32,128,256]{2,1,0:T(8,128)(2,1)} %constant_dynamic-update-slice_fusion.4.lo2), channel_id=1, source_target_pairs={{0,3},{1,2},{2,1},{3,0},{4,36},{5,37},{6,38},{7,39},{8,11},{9,10},... | collective-permute-start | bytes 6291464 | tf_op jit(solution)/shard_map/ppermute | solution.py:250
  80.2 31.7 %all-to-all-start = ((f32[16,4,128]{2,1,0:T(4,128)}), f32[16,4,128]{2,1,0:T(4,128)S(1)}, u32[]{:S(2)}, u32[]{:S(2)}) async-start(f32[16,4,128]{2,1,0:T(4,128)} %bitcast.3), calls=%async_computation | async-start | bytes 65536 | tf_op jit(solution)/shard_map/all_to_all | solution.py:285
  167.6 50.5 %collective-permute-start.21 = (bf16[32,128,384]{2,1,0:T(8,128)(2,1)}, bf16[32,128,384]{2,1,0:T(8,128)(2,1)}, u32[]{:S(2)}, u32[]{:S(2)}) collective-permute-start(bf16[32,128,384]{2,1,0:T(8,128)(2,1)} %scatter_rows.7), channel_id=1, source_target_pairs={{0,24},{1,25},{2,26},{3,27},{4,5},{5,4},{6,7},{7,6},{8,16},{9,17},... | collective-permute-start | bytes 9437192 | tf_op jit(solution)/shard_map/ppermute | solution.py:264
  176.6 50.5 %collective-permute-start.27 = (bf16[32,128,384]{2,1,0:T(8,128)(2,1)S(1)}, bf16[32,128,384]{2,1,0:T(8,128)(2,1)S(1)}, u32[]{:S(2)}, u32[]{:S(2)}) collective-permute-start(bf16[32,128,384]{2,1,0:T(8,128)(2,1)S(1)} %scatter_rows.9), channel_id=1, source_target_pairs={{0,96},{1,97},{2,98},{3,99},{4,12},{5,13},{6,14},{7,15},{8,104},{9... | collective-permute-start | bytes 9437192 | tf_op jit(solution)/shard_map/ppermute | solution.py:264
  180.5 28.8 %collective-permute-start.33 = (bf16[32,128,256]{2,1,0:T(8,128)(2,1)S(1)}, bf16[32,128,256]{2,1,0:T(8,128)(2,1)S(1)}, u32[]{:S(2)}, u32[]{:S(2)}) collective-permute-start(bf16[32,128,256]{2,1,0:T(8,128)(2,1)S(1)} %scatter_rows.11), channel_id=1, source_target_pairs={{0,3},{1,2},{2,1},{3,0},{4,36},{5,37},{6,38},{7,39},{8,11},{9,10},... | collective-permute-start | bytes 6291464 | tf_op jit(solution)/shard_map/ppermute | solution.py:264
  210.0 23.9 %collective-permute-start.34 = (bf16[16,128,256]{2,1,0:T(8,128)(2,1)S(1)}, bf16[16,128,256]{2,1,0:T(8,128)(2,1)S(1)}, u32[]{:S(2)}, u32[]{:S(2)}) collective-permute-start(bf16[16,128,256]{2,1,0:T(8,128)(2,1)S(1)} %get-tuple-element.49), channel_id=1, source_target_pairs={{0,8},{1,9},{2,10},{3,11},{4,7},{5,6},{6,5},{7,4},{8,0},{9,1},{10,... | collective-permute-start | bytes 3145736 | tf_op jit(solution)/shard_map/ppermute | solution.py:264
  221.3 28.5 %collective-permute-start.22 = (bf16[16,128,384]{2,1,0:T(8,128)(2,1)S(1)}, bf16[16,128,384]{2,1,0:T(8,128)(2,1)S(1)}, u32[]{:S(2)}, u32[]{:S(2)}) collective-permute-start(bf16[16,128,384]{2,1,0:T(8,128)(2,1)S(1)} %get-tuple-element.45), channel_id=1, source_target_pairs={{0,32},{1,33},{2,34},{3,35},{4,28},{5,29},{6,30},{7,31},{8,40},{9,... | collective-permute-start | bytes 4718600 | tf_op jit(solution)/shard_map/ppermute | solution.py:264
  228.2 26.0 %collective-permute-start.28 = (bf16[16,128,384]{2,1,0:T(8,128)(2,1)S(1)}, bf16[16,128,384]{2,1,0:T(8,128)(2,1)S(1)}, u32[]{:S(2)}, u32[]{:S(2)}) collective-permute-start(bf16[16,128,384]{2,1,0:T(8,128)(2,1)S(1)} %get-tuple-element.47), channel_id=1, source_target_pairs={{0,1},{1,0},{2,3},{3,2},{4,100},{5,101},{6,102},{7,103},{8,9},{9,8... | collective-permute-start | bytes 4718600 | tf_op jit(solution)/shard_map/ppermute | solution.py:264
  234.2 12.9 %collective-permute-start.35 = (bf16[8,128,256]{2,1,0:T(8,128)(2,1)S(1)}, bf16[8,128,256]{2,1,0:T(8,128)(2,1)S(1)}, u32[]{:S(2)}, u32[]{:S(2)}) collective-permute-start(bf16[8,128,256]{2,1,0:T(8,128)(2,1)S(1)} %get-tuple-element.59), channel_id=1, source_target_pairs={{0,96},{1,97},{2,98},{3,99},{4,12},{5,13},{6,14},{7,15},{8,104},{9... | collective-permute-start | bytes 1572872 | tf_op jit(solution)/shard_map/ppermute | solution.py:264
  247.2 12.6 %collective-permute-start.36 = (bf16[4,128,256]{2,1,0:T(8,128)(2,1)S(1)}, bf16[4,128,256]{2,1,0:T(8,128)(2,1)S(1)}, u32[]{:S(2)}, u32[]{:S(2)}) collective-permute-start(bf16[4,128,256]{2,1,0:T(8,128)(2,1)S(1)} %get-tuple-element.65), channel_id=1, source_target_pairs={{0,1},{1,0},{2,3},{3,2},{4,100},{5,101},{6,102},{7,103},{8,9},{9,8... | collective-permute-start | bytes 786440 | tf_op jit(solution)/shard_map/ppermute | solution.py:264
  250.3 22.5 %collective-permute-start.23 = (bf16[8,128,384]{2,1,0:T(8,128)(2,1)S(1)}, bf16[8,128,384]{2,1,0:T(8,128)(2,1)}, u32[]{:S(2)}, u32[]{:S(2)}) collective-permute-start(bf16[8,128,384]{2,1,0:T(8,128)(2,1)S(1)} %get-tuple-element.51), channel_id=1, source_target_pairs={{0,3},{1,2},{2,1},{3,0},{4,36},{5,37},{6,38},{7,39},{8,11},{9,10},... | collective-permute-start | bytes 2359304 | tf_op jit(solution)/shard_map/ppermute | solution.py:264
  254.7 24.3 %collective-permute-start.29 = (bf16[8,128,384]{2,1,0:T(8,128)(2,1)S(1)}, bf16[8,128,384]{2,1,0:T(8,128)(2,1)}, u32[]{:S(2)}, u32[]{:S(2)}) collective-permute-start(bf16[8,128,384]{2,1,0:T(8,128)(2,1)S(1)} %get-tuple-element.53), channel_id=1, source_target_pairs={{0,24},{1,25},{2,26},{3,27},{4,5},{5,4},{6,7},{7,6},{8,16},{9,17},... | collective-permute-start | bytes 2359304 | tf_op jit(solution)/shard_map/ppermute | solution.py:264
  259.9 10.2 %collective-permute-start.37 = (bf16[2,128,256]{2,1,0:T(8,128)(2,1)S(1)}, bf16[2,128,256]{2,1,0:T(8,128)(2,1)S(1)}, u32[]{:S(2)}, u32[]{:S(2)}) collective-permute-start(bf16[2,128,256]{2,1,0:T(8,128)(2,1)S(1)} %get-tuple-element.71), channel_id=1, source_target_pairs={{0,24},{1,25},{2,26},{3,27},{4,5},{5,4},{6,7},{7,6},{8,16},{9,17},... | collective-permute-start | bytes 393224 | tf_op jit(solution)/shard_map/ppermute | solution.py:264
  270.1 10.3 %collective-permute-start.38 = (bf16[1,128,256]{2,1,0:T(8,128)(2,1)S(1)}, bf16[1,128,256]{2,1,0:T(8,128)(2,1)S(1)}, u32[]{:S(2)}, u32[]{:S(2)}) collective-permute-start(bf16[1,128,256]{2,1,0:T(8,128)(2,1)S(1)} %add_convert_fusion.28), channel_id=1, source_target_pairs={{0,32},{1,33},{2,34},{3,35},{4,28},{5,29},{6,30},{7,31},{8,40},{9,... | collective-permute-start | bytes 196616 | tf_op jit(solution)/shard_map/ppermute | solution.py:264
  274.1 10.7 %collective-permute-start.24 = (bf16[4,128,384]{2,1,0:T(8,128)(2,1)S(1)}, bf16[4,128,384]{2,1,0:T(8,128)(2,1)S(1)}, u32[]{:S(2)}, u32[]{:S(2)}) collective-permute-start(bf16[4,128,384]{2,1,0:T(8,128)(2,1)S(1)} %get-tuple-element.61), channel_id=1, source_target_pairs={{0,8},{1,9},{2,10},{3,11},{4,7},{5,6},{6,5},{7,4},{8,0},{9,1},{10,... | collective-permute-start | bytes 1179656 | tf_op jit(solution)/shard_map/ppermute | solution.py:264
  280.3 25.8 %copy-start.4 = (bf16[128,1024]{1,0:T(8,128)(2,1)S(1)}, bf16[128,1024]{1,0:T(8,128)(2,1)}, u32[]{:S(2)}) copy-start(bf16[128,1024]{1,0:T(8,128)(2,1)} %param.14) | copy-start | bytes 786436
  280.3 10.0 %collective-permute-start.30 = (bf16[4,128,384]{2,1,0:T(8,128)(2,1)S(1)}, bf16[4,128,384]{2,1,0:T(8,128)(2,1)S(1)}, u32[]{:S(2)}, u32[]{:S(2)}) collective-permute-start(bf16[4,128,384]{2,1,0:T(8,128)(2,1)S(1)} %get-tuple-element.63), channel_id=1, source_target_pairs={{0,32},{1,33},{2,34},{3,35},{4,28},{5,29},{6,30},{7,31},{8,40},{9,... | collective-permute-start | bytes 1179656 | tf_op jit(solution)/shard_map/ppermute | solution.py:264
  284.9 26.1 %copy-start.3 = (bf16[4096,256]{1,0:T(8,128)(2,1)S(1)}, bf16[4096,256]{1,0:T(8,128)(2,1)}, u32[]{:S(2)}) copy-start(bf16[4096,256]{1,0:T(8,128)(2,1)} %param.22) | copy-start | bytes 6291460
  284.9 9.1 %collective-permute-start.25 = (bf16[2,128,384]{2,1,0:T(8,128)(2,1)S(1)}, bf16[2,128,384]{2,1,0:T(8,128)(2,1)S(1)}, u32[]{:S(2)}, u32[]{:S(2)}) collective-permute-start(bf16[2,128,384]{2,1,0:T(8,128)(2,1)S(1)} %get-tuple-element.67), channel_id=1, source_target_pairs={{0,96},{1,97},{2,98},{3,99},{4,12},{5,13},{6,14},{7,15},{8,104},{9... | collective-permute-start | bytes 589832 | tf_op jit(solution)/shard_map/ppermute | solution.py:264
  290.4 9.3 %collective-permute-start.31 = (bf16[2,128,384]{2,1,0:T(8,128)(2,1)S(1)}, bf16[2,128,384]{2,1,0:T(8,128)(2,1)S(1)}, u32[]{:S(2)}, u32[]{:S(2)}) collective-permute-start(bf16[2,128,384]{2,1,0:T(8,128)(2,1)S(1)} %get-tuple-element.69), channel_id=1, source_target_pairs={{0,3},{1,2},{2,1},{3,0},{4,36},{5,37},{6,38},{7,39},{8,11},{9,10},... | collective-permute-start | bytes 589832 | tf_op jit(solution)/shard_map/ppermute | solution.py:264
  294.0 9.4 %collective-permute-start.26 = (bf16[1,128,384]{2,1,0:T(8,128)(2,1)S(1)}, bf16[1,128,384]{2,1,0:T(8,128)(2,1)S(1)}, u32[]{:S(2)}, u32[]{:S(2)}) collective-permute-start(bf16[1,128,384]{2,1,0:T(8,128)(2,1)S(1)} %add_convert_fusion.26), channel_id=1, source_target_pairs={{0,1},{1,0},{2,3},{3,2},{4,100},{5,101},{6,102},{7,103},{8,9},{9,8... | collective-permute-start | bytes 294920 | tf_op jit(solution)/shard_map/ppermute | solution.py:264
  299.8 6.2 %collective-permute-start.32 = (bf16[1,128,384]{2,1,0:T(8,128)(2,1)S(1)}, bf16[1,128,384]{2,1,0:T(8,128)(2,1)S(1)}, u32[]{:S(2)}, u32[]{:S(2)}) collective-permute-start(bf16[1,128,384]{2,1,0:T(8,128)(2,1)S(1)} %add_convert_fusion.24), channel_id=1, source_target_pairs={{0,8},{1,9},{2,10},{3,11},{4,7},{5,6},{6,5},{7,4},{8,0},{9,1},{10,... | collective-permute-start | bytes 294920 | tf_op jit(solution)/shard_map/ppermute | solution.py:264
  306.2 6.5 %collective-permute-start.39 = (bf16[128,1024]{1,0:T(8,128)(2,1)S(1)}, bf16[128,1024]{1,0:T(8,128)(2,1)S(1)}, u32[]{:S(2)}, u32[]{:S(2)}) collective-permute-start(bf16[128,1024]{1,0:T(8,128)(2,1)S(1)} %fusion.22), channel_id=1, source_target_pairs={{0,1},{1,0},{2,3},{3,2},{4,5},{5,4},{6,7},{7,6},{8,9},{9,8},{10,11... | collective-permute-start | bytes 786440 | tf_op jit(solution)/shard_map/ppermute | solution.py:320
  306.3 9.0 %collective-permute-start.40 = (bf16[128,1024]{1,0:T(8,128)(2,1)S(1)}, bf16[128,1024]{1,0:T(8,128)(2,1)S(1)}, u32[]{:S(2)}, u32[]{:S(2)}) collective-permute-start(bf16[128,1024]{1,0:T(8,128)(2,1)S(1)} %fusion.22), channel_id=1, source_target_pairs={{0,2},{1,3},{2,0},{3,1},{4,6},{5,7},{6,4},{7,5},{8,10},{9,11},{10,... | collective-permute-start | bytes 786440 | tf_op jit(solution)/shard_map/ppermute | solution.py:320
  308.0 10.0 %collective-permute-start.41 = (bf16[128,1024]{1,0:T(8,128)(2,1)S(1)}, bf16[128,1024]{1,0:T(8,128)(2,1)S(1)}, u32[]{:S(2)}, u32[]{:S(2)}) collective-permute-start(bf16[128,1024]{1,0:T(8,128)(2,1)S(1)} %fusion.22), channel_id=1, source_target_pairs={{0,3},{1,2},{2,1},{3,0},{4,7},{5,6},{6,5},{7,4},{8,11},{9,10},{10,... | collective-permute-start | bytes 786440 | tf_op jit(solution)/shard_map/ppermute | solution.py:320
  (14 other events, 136.9 us)
